TPU v7x, 512 devices: a whole 4x4x16 slice. The times are simulated.
512 devices in a mesh: dp: 512 (over z, y, x, core).
Axes of the slice: x: 4, y: 4, z: 16, core: 2. Of those that a mesh axis runs over, the one named last changes fastest.
Arguments:
- picture_vectors: bfloat16 [131072, 1152], P('dp'), may hold values from -0.19921875 to 0.19921875
- caption_vectors: bfloat16 [131072, 1152], P('dp'), may hold values from -0.19921875 to 0.19921875
- sharpness_factor: float32 [1], replicated, may hold values from 4 to 12
- affinity_offset: float32 [1], replicated, may hold values from -3 to -1
Outputs:
- loss_rows: float32 [131072], P('dp')
- image_embedding_gradient: float32 [131072, 1152], P('dp')
- text_grad: float32 [131072, 1152], P('dp')
All inputs are finite; a program needn't handle non-finite values.
Results may differ from a plain program's by a relative error of at most 0.0043.
Values may be sent and summed in bfloat16 or wider, within the bound.
A program may use at most 64 MiB of HBM per device.

v0:
```python
import jax
import jax.numpy as jnp
from jax import lax
from jax.sharding import PartitionSpec as P

STEPS = 8


def from_behind(block, axis, distance):
    devices = range(lax.axis_size(axis))
    route = [((i - distance) % len(devices), i) for i in devices]
    return lax.ppermute(block, axis, route)


def normed(values):
    full = values.astype(jnp.float32)
    length = jnp.sqrt(jnp.sum(full * full, axis=1, keepdims=True) + 1e-06)
    return (full / length, length)


def slopes(img_b, txt_block, similarity_multiplier, offset, step):
    rows = img_b.shape[0]
    similarity_matrix = lax.dot_general(
        img_b, txt_block, (((1,), (1,)), ((), ())), preferred_element_type=jnp.float32
    )
    logits = similarity_multiplier * similarity_matrix + offset
    if step == 0:
        same = lax.broadcasted_iota(jnp.int32, (rows, rows), 0) == lax.broadcasted_iota(
            jnp.int32, (rows, rows), 1
        )
        label = jnp.where(same, 1.0, -1.0).astype(jnp.float32)
    else:
        label = jnp.full((rows, rows), -1.0, jnp.float32)
    row_loss = jnp.sum(jax.nn.softplus(-label * logits), axis=1)
    slope = (-label * jax.nn.sigmoid(-label * logits)).astype(jnp.bfloat16)
    return (row_loss, slope)


def image_side(slope, txt_block, similarity_multiplier):
    return similarity_multiplier * jnp.dot(slope, txt_block, preferred_element_type=jnp.float32)


def text_side(slope, img_b, similarity_multiplier):
    return similarity_multiplier * lax.dot_general(
        slope, img_b, (((0,), (0,)), ((), ())), preferred_element_type=jnp.float32
    )


def pairwise_terms(img_b, txt_block, similarity_multiplier, offset, step):
    row_loss, slope = slopes(img_b, txt_block, similarity_multiplier, offset, step)
    return (
        row_loss,
        image_side(slope, txt_block, similarity_multiplier),
        text_side(slope, img_b, similarity_multiplier),
    )


def on_device(picture_vectors, caption_vectors, sharpness_factor, affinity_offset):
    img_unit, image_norm_values = normed(picture_vectors)
    txt_unit, text_norm_values = normed(caption_vectors)
    img_b = img_unit.astype(jnp.bfloat16)
    txt_b = txt_unit.astype(jnp.bfloat16)
    similarity_multiplier = sharpness_factor[0]
    offset = affinity_offset[0]
    rows = picture_vectors.shape[0]
    loss_sum = jnp.zeros((rows,), jnp.float32)
    image_normalized = jnp.zeros(picture_vectors.shape, jnp.float32)
    block = txt_b
    carried = jnp.zeros(caption_vectors.shape, jnp.float32)
    for step in range(STEPS):
        if step > 0:
            block = from_behind(block, "dp", 1)
            carried = from_behind(carried, "dp", 1)
        row_loss, img_part, text_portion = pairwise_terms(
            img_b, block, similarity_multiplier, offset, step
        )
        loss_sum = loss_sum + row_loss
        image_normalized = image_normalized + img_part
        carried = carried + text_portion
    txt_hat = from_behind(carried, "dp", -(STEPS - 1))
    loss_rows = loss_sum / (STEPS * rows)
    image_embedding_gradient = (
        image_normalized - img_unit * jnp.sum(img_unit * image_normalized, axis=1, keepdims=True)
    ) / image_norm_values
    text_grad = (
        txt_hat - txt_unit * jnp.sum(txt_unit * txt_hat, axis=1, keepdims=True)
    ) / text_norm_values
    return (loss_rows, image_embedding_gradient, text_grad)


def solution(mesh):
    placed = (P("dp", None), P("dp", None), P(), P())
    return jax.shard_map(
        on_device,
        mesh=mesh,
        in_specs=placed,
        out_specs=(P("dp"), P("dp", None), P("dp", None)),
        check_vma=False,
    )
```

profile of v0, /device:TPU:6, one launch (start us, length us, event | category | flops | bytes accessed | tf_op | source)
XLA Modules:
  0.0 243.9 jit_solution(15694744917380027953)
XLA Ops:
  1.3 1.3 fusion.2
  2.6 1.3 fusion.21
  3.9 0.2 fusion.3
  4.1 0.2 fusion.22
  5.0 0.5 fusion.13
  5.5 0.4 convolution_multiply_fusion.7
  5.9 1.9 collective-permute-start.7
  7.8 3.5 %collective-permute-start = (bf16[256,1152]{1,0:T(8,128)(2,1)S(1)}, bf16[256,1152]{1,0:T(8,128)(2,1)S(1)}, u32[]{:S(2)}, u32[]{:S(2)}) collective-permute-start(bf16[256,1152]{1,0:T(8,128)(2,1)S(1)} %fusion.22), channel_id=1, source_target_pairs={{511,0},{0,1},{1,2},{2,3},{3,4},{4,5},{5,6},{6,7},{7,8},{8,9},{9,1... | collective-permute-start | bytes 1769480 | tf_op jit(solution)/shard_map/ppermute | solution.py:12
  11.3 18.4 %collective-permute-done = bf16[256,1152]{1,0:T(8,128)(2,1)S(1)} collective-permute-done((bf16[256,1152]{1,0:T(8,128)(2,1)S(1)}, bf16[256,1152]{1,0:T(8,128)(2,1)S(1)}, u32[]{:S(2)}, u32[]{:S(2)}) %collective-permute-start) | collective-permute-done | bytes 589856 | tf_op jit(solution)/shard_map/ppermute | solution.py:12
  29.8 0.5 fusion.14
  30.3 0.4 fusion.1
  30.6 1.9 collective-permute-start.8
  32.6 5.6 %collective-permute-start.1 = (bf16[256,1152]{1,0:T(8,128)(2,1)S(1)}, bf16[256,1152]{1,0:T(8,128)(2,1)S(1)}, u32[]{:S(2)}, u32[]{:S(2)}) collective-permute-start(bf16[256,1152]{1,0:T(8,128)(2,1)S(1)} %collective-permute-done), channel_id=1, source_target_pairs={{511,0},{0,1},{1,2},{2,3},{3,4},{4,5},{5,6},{6,7},{7,8},{8,9},{9,1... | collective-permute-start | bytes 1769480 | tf_op jit(solution)/shard_map/ppermute | solution.py:12
  38.2 16.3 %collective-permute-done.1 = bf16[256,1152]{1,0:T(8,128)(2,1)S(1)} collective-permute-done((bf16[256,1152]{1,0:T(8,128)(2,1)S(1)}, bf16[256,1152]{1,0:T(8,128)(2,1)S(1)}, u32[]{:S(2)}, u32[]{:S(2)}) %collective-permute-start.1) | collective-permute-done | bytes 589856 | tf_op jit(solution)/shard_map/ppermute | solution.py:12
  54.5 0.5 fusion.15
  55.0 0.4 convolution_multiply_fusion.5
  55.4 0.1 add.204
  55.5 3.2 %collective-permute-start.9 = (f32[256,1152]{1,0:T(8,128)S(1)}, f32[256,1152]{1,0:T(8,128)S(1)}, u32[]{:S(2)}, u32[]{:S(2)}) collective-permute-start(f32[256,1152]{1,0:T(8,128)S(1)} %add.204), channel_id=1, source_target_pairs={{511,0},{0,1},{1,2},{2,3},{3,4},{4,5},{5,6},{6,7},{7,8},{8,9},{9,1... | collective-permute-start | bytes 3538952 | tf_op jit(solution)/shard_map/ppermute | solution.py:12
  58.6 6.5 %collective-permute-start.2 = (bf16[256,1152]{1,0:T(8,128)(2,1)S(1)}, bf16[256,1152]{1,0:T(8,128)(2,1)S(1)}, u32[]{:S(2)}, u32[]{:S(2)}) collective-permute-start(bf16[256,1152]{1,0:T(8,128)(2,1)S(1)} %collective-permute-done.1), channel_id=1, source_target_pairs={{511,0},{0,1},{1,2},{2,3},{3,4},{4,5},{5,6},{6,7},{7,8},{8,9},{9,1... | collective-permute-start | bytes 1769480 | tf_op jit(solution)/shard_map/ppermute | solution.py:12
  65.1 14.2 %collective-permute-done.2 = bf16[256,1152]{1,0:T(8,128)(2,1)S(1)} collective-permute-done((bf16[256,1152]{1,0:T(8,128)(2,1)S(1)}, bf16[256,1152]{1,0:T(8,128)(2,1)S(1)}, u32[]{:S(2)}, u32[]{:S(2)}) %collective-permute-start.2) | collective-permute-done | bytes 589856 | tf_op jit(solution)/shard_map/ppermute | solution.py:12
  79.3 0.5 fusion.16
  79.8 0.4 convolution_multiply_fusion.4
  80.2 0.0 collective-permute-done.9
  80.2 0.1 add.205
  80.3 5.2 %collective-permute-start.10 = (f32[256,1152]{1,0:T(8,128)S(1)}, f32[256,1152]{1,0:T(8,128)S(1)}, u32[]{:S(2)}, u32[]{:S(2)}) collective-permute-start(f32[256,1152]{1,0:T(8,128)S(1)} %add.205), channel_id=1, source_target_pairs={{511,0},{0,1},{1,2},{2,3},{3,4},{4,5},{5,6},{6,7},{7,8},{8,9},{9,1... | collective-permute-start | bytes 3538952 | tf_op jit(solution)/shard_map/ppermute | solution.py:12
  85.6 6.5 %collective-permute-start.3 = (bf16[256,1152]{1,0:T(8,128)(2,1)S(1)}, bf16[256,1152]{1,0:T(8,128)(2,1)S(1)}, u32[]{:S(2)}, u32[]{:S(2)}) collective-permute-start(bf16[256,1152]{1,0:T(8,128)(2,1)S(1)} %collective-permute-done.2), channel_id=1, source_target_pairs={{511,0},{0,1},{1,2},{2,3},{3,4},{4,5},{5,6},{6,7},{7,8},{8,9},{9,1... | collective-permute-start | bytes 1769480 | tf_op jit(solution)/shard_map/ppermute | solution.py:12
  92.1 12.1 %collective-permute-done.3 = bf16[256,1152]{1,0:T(8,128)(2,1)S(1)} collective-permute-done((bf16[256,1152]{1,0:T(8,128)(2,1)S(1)}, bf16[256,1152]{1,0:T(8,128)(2,1)S(1)}, u32[]{:S(2)}, u32[]{:S(2)}) %collective-permute-start.3) | collective-permute-done | bytes 589856 | tf_op jit(solution)/shard_map/ppermute | solution.py:12
  104.2 0.5 fusion.17
  104.7 0.4 convolution_multiply_fusion.3
  105.1 0.1 add.206
  105.2 7.4 %collective-permute-start.11 = (f32[256,1152]{1,0:T(8,128)S(1)}, f32[256,1152]{1,0:T(8,128)S(1)}, u32[]{:S(2)}, u32[]{:S(2)}) collective-permute-start(f32[256,1152]{1,0:T(8,128)S(1)} %add.206), channel_id=1, source_target_pairs={{511,0},{0,1},{1,2},{2,3},{3,4},{4,5},{5,6},{6,7},{7,8},{8,9},{9,1... | collective-permute-start | bytes 3538952 | tf_op jit(solution)/shard_map/ppermute | solution.py:12
  112.6 6.5 %collective-permute-start.4 = (bf16[256,1152]{1,0:T(8,128)(2,1)S(1)}, bf16[256,1152]{1,0:T(8,128)(2,1)S(1)}, u32[]{:S(2)}, u32[]{:S(2)}) collective-permute-start(bf16[256,1152]{1,0:T(8,128)(2,1)S(1)} %collective-permute-done.3), channel_id=1, source_target_pairs={{511,0},{0,1},{1,2},{2,3},{3,4},{4,5},{5,6},{6,7},{7,8},{8,9},{9,1... | collective-permute-start | bytes 1769480 | tf_op jit(solution)/shard_map/ppermute | solution.py:12
  119.1 0.4 fusion.23
  119.5 9.5 %collective-permute-done.4 = bf16[256,1152]{1,0:T(8,128)(2,1)S(1)} collective-permute-done((bf16[256,1152]{1,0:T(8,128)(2,1)S(1)}, bf16[256,1152]{1,0:T(8,128)(2,1)S(1)}, u32[]{:S(2)}, u32[]{:S(2)}) %collective-permute-start.4) | collective-permute-done | bytes 589856 | tf_op jit(solution)/shard_map/ppermute | solution.py:12
  129.0 0.5 fusion.18
  129.5 0.4 convolution_multiply_fusion.2
  129.9 0.0 collective-permute-done.11
  129.9 0.1 add.207
  130.0 9.5 %collective-permute-start.12 = (f32[256,1152]{1,0:T(8,128)S(1)}, f32[256,1152]{1,0:T(8,128)S(1)}, u32[]{:S(2)}, u32[]{:S(2)}) collective-permute-start(f32[256,1152]{1,0:T(8,128)S(1)} %add.207), channel_id=1, source_target_pairs={{511,0},{0,1},{1,2},{2,3},{3,4},{4,5},{5,6},{6,7},{7,8},{8,9},{9,1... | collective-permute-start | bytes 3538952 | tf_op jit(solution)/shard_map/ppermute | solution.py:12
  139.5 0.4 convolution_add_fusion.6
  139.9 6.5 %collective-permute-start.5 = (bf16[256,1152]{1,0:T(8,128)(2,1)S(1)}, bf16[256,1152]{1,0:T(8,128)(2,1)S(1)}, u32[]{:S(2)}, u32[]{:S(2)}) collective-permute-start(bf16[256,1152]{1,0:T(8,128)(2,1)S(1)} %collective-permute-done.4), channel_id=1, source_target_pairs={{511,0},{0,1},{1,2},{2,3},{3,4},{4,5},{5,6},{6,7},{7,8},{8,9},{9,1... | collective-permute-start | bytes 1769480 | tf_op jit(solution)/shard_map/ppermute | solution.py:12
  146.4 0.4 convolution_add_fusion.5
  146.9 0.4 convolution_add_fusion.4
  147.3 6.6 %collective-permute-done.5 = bf16[256,1152]{1,0:T(8,128)(2,1)S(1)} collective-permute-done((bf16[256,1152]{1,0:T(8,128)(2,1)S(1)}, bf16[256,1152]{1,0:T(8,128)(2,1)S(1)}, u32[]{:S(2)}, u32[]{:S(2)}) %collective-permute-start.5) | collective-permute-done | bytes 589856 | tf_op jit(solution)/shard_map/ppermute | solution.py:12
  153.9 0.5 fusion.19
  154.4 0.4 convolution_multiply_fusion.1
  154.8 0.1 add.208
  154.9 11.6 %collective-permute-start.13 = (f32[256,1152]{1,0:T(8,128)S(1)}, f32[256,1152]{1,0:T(8,128)S(1)}, u32[]{:S(2)}, u32[]{:S(2)}) collective-permute-start(f32[256,1152]{1,0:T(8,128)S(1)} %add.208), channel_id=1, source_target_pairs={{511,0},{0,1},{1,2},{2,3},{3,4},{4,5},{5,6},{6,7},{7,8},{8,9},{9,1... | collective-permute-start | bytes 3538952 | tf_op jit(solution)/shard_map/ppermute | solution.py:12
  166.5 0.4 convolution_add_fusion.3
  166.9 6.7 %collective-permute-start.6 = (bf16[256,1152]{1,0:T(8,128)(2,1)S(1)}, bf16[256,1152]{1,0:T(8,128)(2,1)S(1)}, u32[]{:S(2)}, u32[]{:S(2)}) collective-permute-start(bf16[256,1152]{1,0:T(8,128)(2,1)S(1)} %collective-permute-done.5), channel_id=1, source_target_pairs={{511,0},{0,1},{1,2},{2,3},{3,4},{4,5},{5,6},{6,7},{7,8},{8,9},{9,1... | collective-permute-start | bytes 1769480 | tf_op jit(solution)/shard_map/ppermute | solution.py:12
  173.6 0.4 convolution_add_fusion.2
  174.0 0.4 convolution_add_fusion.1
  174.4 4.3 %collective-permute-done.6 = bf16[256,1152]{1,0:T(8,128)(2,1)S(1)} collective-permute-done((bf16[256,1152]{1,0:T(8,128)(2,1)S(1)}, bf16[256,1152]{1,0:T(8,128)(2,1)S(1)}, u32[]{:S(2)}, u32[]{:S(2)}) %collective-permute-start.6) | collective-permute-done | bytes 589856 | tf_op jit(solution)/shard_map/ppermute | solution.py:12
  178.7 0.5 fusion.20
  179.2 0.4 convolution_multiply_fusion
  179.6 0.0 copy-start.1
  179.6 0.1 add.209
  179.8 43.6 %collective-permute-start.14 = (f32[256,1152]{1,0:T(8,128)S(1)}, f32[256,1152]{1,0:T(8,128)S(1)}, u32[]{:S(2)}, u32[]{:S(2)}) collective-permute-start(f32[256,1152]{1,0:T(8,128)S(1)} %add.209), channel_id=1, source_target_pairs={{7,0},{8,1},{9,2},{10,3},{11,4},{12,5},{13,6},{14,7},{15,8},{16,9}... | collective-permute-start | bytes 3538952 | tf_op jit(solution)/shard_map/ppermute | solution.py:12
  223.4 0.6 add_multiply_fusion
  223.9 0.5 multiply_reduce_fusion.1
  224.5 1.3 subtract_divide_fusion.1
  225.8 16.5 %collective-permute-done.14 = f32[256,1152]{1,0:T(8,128)S(1)} collective-permute-done((f32[256,1152]{1,0:T(8,128)S(1)}, f32[256,1152]{1,0:T(8,128)S(1)}, u32[]{:S(2)}, u32[]{:S(2)}) %collective-permute-start.14) | collective-permute-done | bytes 1179680 | tf_op jit(solution)/shard_map/ppermute | solution.py:12
  242.3 0.3 multiply_reduce_fusion
  242.6 1.3 subtract_divide_fusion
  (10 shorter events, 0.0 us)
Async XLA Ops:
  0.6 3.3 %copy-start = (bf16[256,1152]{1,0:T(8,128)(2,1)S(1)}, bf16[256,1152]{1,0:T(8,128)(2,1)}, u32[]{:S(2)}) copy-start(bf16[256,1152]{1,0:T(8,128)(2,1)} %param.5) | copy-start | bytes 1769476
  5.9 24.3 %collective-permute-start.7 = (f32[256,1152]{1,0:T(8,128)S(1)}, f32[256,1152]{1,0:T(8,128)S(1)}, u32[]{:S(2)}, u32[]{:S(2)}) collective-permute-start(f32[256,1152]{1,0:T(8,128)S(1)} %convolution_multiply_fusion.7), channel_id=1, source_target_pairs={{511,0},{0,1},{1,2},{2,3},{3,4},{4,5},{5,6},{6,7},{7,8},{8,9},{9,1... | collective-permute-start | bytes 3538952 | tf_op jit(solution)/shard_map/ppermute | solution.py:12
  7.8 21.9 %collective-permute-start = (bf16[256,1152]{1,0:T(8,128)(2,1)S(1)}, bf16[256,1152]{1,0:T(8,128)(2,1)S(1)}, u32[]{:S(2)}, u32[]{:S(2)}) collective-permute-start(bf16[256,1152]{1,0:T(8,128)(2,1)S(1)} %fusion.22), channel_id=1, source_target_pairs={{511,0},{0,1},{1,2},{2,3},{3,4},{4,5},{5,6},{6,7},{7,8},{8,9},{9,1... | collective-permute-start | bytes 1769480 | tf_op jit(solution)/shard_map/ppermute | solution.py:12
  30.6 24.7 %collective-permute-start.8 = (f32[256,1152]{1,0:T(8,128)S(1)}, f32[256,1152]{1,0:T(8,128)S(1)}, u32[]{:S(2)}, u32[]{:S(2)}) collective-permute-start(f32[256,1152]{1,0:T(8,128)S(1)} %fusion.1), channel_id=1, source_target_pairs={{511,0},{0,1},{1,2},{2,3},{3,4},{4,5},{5,6},{6,7},{7,8},{8,9},{9,1... | collective-permute-start | bytes 3538952 | tf_op jit(solution)/shard_map/ppermute | solution.py:12
  32.6 21.9 %collective-permute-start.1 = (bf16[256,1152]{1,0:T(8,128)(2,1)S(1)}, bf16[256,1152]{1,0:T(8,128)(2,1)S(1)}, u32[]{:S(2)}, u32[]{:S(2)}) collective-permute-start(bf16[256,1152]{1,0:T(8,128)(2,1)S(1)} %collective-permute-done), channel_id=1, source_target_pairs={{511,0},{0,1},{1,2},{2,3},{3,4},{4,5},{5,6},{6,7},{7,8},{8,9},{9,1... | collective-permute-start | bytes 1769480 | tf_op jit(solution)/shard_map/ppermute | solution.py:12
  55.5 24.7 %collective-permute-start.9 = (f32[256,1152]{1,0:T(8,128)S(1)}, f32[256,1152]{1,0:T(8,128)S(1)}, u32[]{:S(2)}, u32[]{:S(2)}) collective-permute-start(f32[256,1152]{1,0:T(8,128)S(1)} %add.204), channel_id=1, source_target_pairs={{511,0},{0,1},{1,2},{2,3},{3,4},{4,5},{5,6},{6,7},{7,8},{8,9},{9,1... | collective-permute-start | bytes 3538952 | tf_op jit(solution)/shard_map/ppermute | solution.py:12
  58.6 20.7 %collective-permute-start.2 = (bf16[256,1152]{1,0:T(8,128)(2,1)S(1)}, bf16[256,1152]{1,0:T(8,128)(2,1)S(1)}, u32[]{:S(2)}, u32[]{:S(2)}) collective-permute-start(bf16[256,1152]{1,0:T(8,128)(2,1)S(1)} %collective-permute-done.1), channel_id=1, source_target_pairs={{511,0},{0,1},{1,2},{2,3},{3,4},{4,5},{5,6},{6,7},{7,8},{8,9},{9,1... | collective-permute-start | bytes 1769480 | tf_op jit(solution)/shard_map/ppermute | solution.py:12
  80.3 24.7 %collective-permute-start.10 = (f32[256,1152]{1,0:T(8,128)S(1)}, f32[256,1152]{1,0:T(8,128)S(1)}, u32[]{:S(2)}, u32[]{:S(2)}) collective-permute-start(f32[256,1152]{1,0:T(8,128)S(1)} %add.205), channel_id=1, source_target_pairs={{511,0},{0,1},{1,2},{2,3},{3,4},{4,5},{5,6},{6,7},{7,8},{8,9},{9,1... | collective-permute-start | bytes 3538952 | tf_op jit(solution)/shard_map/ppermute | solution.py:12
  85.6 18.6 %collective-permute-start.3 = (bf16[256,1152]{1,0:T(8,128)(2,1)S(1)}, bf16[256,1152]{1,0:T(8,128)(2,1)S(1)}, u32[]{:S(2)}, u32[]{:S(2)}) collective-permute-start(bf16[256,1152]{1,0:T(8,128)(2,1)S(1)} %collective-permute-done.2), channel_id=1, source_target_pairs={{511,0},{0,1},{1,2},{2,3},{3,4},{4,5},{5,6},{6,7},{7,8},{8,9},{9,1... | collective-permute-start | bytes 1769480 | tf_op jit(solution)/shard_map/ppermute | solution.py:12
  105.2 24.7 %collective-permute-start.11 = (f32[256,1152]{1,0:T(8,128)S(1)}, f32[256,1152]{1,0:T(8,128)S(1)}, u32[]{:S(2)}, u32[]{:S(2)}) collective-permute-start(f32[256,1152]{1,0:T(8,128)S(1)} %add.206), channel_id=1, source_target_pairs={{511,0},{0,1},{1,2},{2,3},{3,4},{4,5},{5,6},{6,7},{7,8},{8,9},{9,1... | collective-permute-start | bytes 3538952 | tf_op jit(solution)/shard_map/ppermute | solution.py:12
  112.6 16.5 %collective-permute-start.4 = (bf16[256,1152]{1,0:T(8,128)(2,1)S(1)}, bf16[256,1152]{1,0:T(8,128)(2,1)S(1)}, u32[]{:S(2)}, u32[]{:S(2)}) collective-permute-start(bf16[256,1152]{1,0:T(8,128)(2,1)S(1)} %collective-permute-done.3), channel_id=1, source_target_pairs={{511,0},{0,1},{1,2},{2,3},{3,4},{4,5},{5,6},{6,7},{7,8},{8,9},{9,1... | collective-permute-start | bytes 1769480 | tf_op jit(solution)/shard_map/ppermute | solution.py:12
  130.0 24.7 %collective-permute-start.12 = (f32[256,1152]{1,0:T(8,128)S(1)}, f32[256,1152]{1,0:T(8,128)S(1)}, u32[]{:S(2)}, u32[]{:S(2)}) collective-permute-start(f32[256,1152]{1,0:T(8,128)S(1)} %add.207), channel_id=1, source_target_pairs={{511,0},{0,1},{1,2},{2,3},{3,4},{4,5},{5,6},{6,7},{7,8},{8,9},{9,1... | collective-permute-start | bytes 3538952 | tf_op jit(solution)/shard_map/ppermute | solution.py:12
  139.9 13.9 %collective-permute-start.5 = (bf16[256,1152]{1,0:T(8,128)(2,1)S(1)}, bf16[256,1152]{1,0:T(8,128)(2,1)S(1)}, u32[]{:S(2)}, u32[]{:S(2)}) collective-permute-start(bf16[256,1152]{1,0:T(8,128)(2,1)S(1)} %collective-permute-done.4), channel_id=1, source_target_pairs={{511,0},{0,1},{1,2},{2,3},{3,4},{4,5},{5,6},{6,7},{7,8},{8,9},{9,1... | collective-permute-start | bytes 1769480 | tf_op jit(solution)/shard_map/ppermute | solution.py:12
  154.9 24.7 %collective-permute-start.13 = (f32[256,1152]{1,0:T(8,128)S(1)}, f32[256,1152]{1,0:T(8,128)S(1)}, u32[]{:S(2)}, u32[]{:S(2)}) collective-permute-start(f32[256,1152]{1,0:T(8,128)S(1)} %add.208), channel_id=1, source_target_pairs={{511,0},{0,1},{1,2},{2,3},{3,4},{4,5},{5,6},{6,7},{7,8},{8,9},{9,1... | collective-permute-start | bytes 3538952 | tf_op jit(solution)/shard_map/ppermute | solution.py:12
  166.9 11.8 %collective-permute-start.6 = (bf16[256,1152]{1,0:T(8,128)(2,1)S(1)}, bf16[256,1152]{1,0:T(8,128)(2,1)S(1)}, u32[]{:S(2)}, u32[]{:S(2)}) collective-permute-start(bf16[256,1152]{1,0:T(8,128)(2,1)S(1)} %collective-permute-done.5), channel_id=1, source_target_pairs={{511,0},{0,1},{1,2},{2,3},{3,4},{4,5},{5,6},{6,7},{7,8},{8,9},{9,1... | collective-permute-start | bytes 1769480 | tf_op jit(solution)/shard_map/ppermute | solution.py:12
  179.6 44.3 %copy-start.1 = (bf16[256,1152]{1,0:T(8,128)(2,1)S(1)}, bf16[256,1152]{1,0:T(8,128)(2,1)}, u32[]{:S(2)}) copy-start(bf16[256,1152]{1,0:T(8,128)(2,1)} %param.4) | copy-start | bytes 1769476
  179.8 62.5 %collective-permute-start.14 = (f32[256,1152]{1,0:T(8,128)S(1)}, f32[256,1152]{1,0:T(8,128)S(1)}, u32[]{:S(2)}, u32[]{:S(2)}) collective-permute-start(f32[256,1152]{1,0:T(8,128)S(1)} %add.209), channel_id=1, source_target_pairs={{7,0},{8,1},{9,2},{10,3},{11,4},{12,5},{13,6},{14,7},{15,8},{16,9}... | collective-permute-start | bytes 3538952 | tf_op jit(solution)/shard_map/ppermute | solution.py:12
where the time goes:
time: 244 us
  starting transfers between devices  126 us (52%)
  waiting for transfers between devices  97.9 us (40%)
  matrix products  10.3 us (4%)
  other arithmetic  7.2 us (3%)
    ppermute x15, starting transfers between devices, from_behind(): return lax.ppermute(block, axis, route)  126 us
    ppermute x15, waiting for transfers between devices, from_behind(): return lax.ppermute(block, axis, route)  97.9 us
  transfers between devices with their start and end apart: 15, of which 8 were waited for; matrix products, arithmetic and copies ran while one was open for 4% of the time, Pallas kernels for 0%

commit v1 on v0

v1 whole, which is shorter than its diff:
```python
import functools

import jax
import jax.numpy as jnp
from jax import lax
from jax.experimental import pallas as pl
from jax.experimental.pallas import tpu as pltpu
from jax.sharding import PartitionSpec as P

STAGES = 4
CHUNKS = 2
LANES = 384
STRIP = 32
MESH = pl.DeviceIdType.MESH


def kernel(s_ref, b_ref, img_ref, txt_ref, loss_ref, gi_ref, gt_ref,
           own, buf, hat, losses, chain_s, chain_r, side_s, side_r):
    rows, depth = img_ref.shape
    part = rows // CHUNKS
    n = lax.axis_index("dp")
    total = lax.axis_size("dp")
    core = lax.rem(n, 2)

    def at(offset):
        return lax.rem(n + offset + total, total)

    sibling = at(1 - 2 * core)
    chain_to = (at(2), at(-2))
    first_to = (at(1 + 6 * core), at(-7 + 6 * core))
    far = at(-7 + 14 * core)

    def chain(kind, stage, chunk):
        source = buf.at[kind, stage, chunk, pl.ds(0, part)]
        return pltpu.make_async_remote_copy(
            src_ref=source,
            dst_ref=buf.at[kind, jnp.minimum(stage + 1, STAGES - 1), chunk, pl.ds(0, part)],
            send_sem=chain_s.at[kind, stage, chunk],
            recv_sem=chain_r.at[kind, stage, chunk],
            device_id=(chain_to[kind],),
            device_id_type=MESH,
        )

    def across(kind, stage, chunk, target):
        return pltpu.make_async_remote_copy(
            src_ref=buf.at[kind, stage, chunk, pl.ds(0, part)],
            dst_ref=buf.at[kind, stage, chunk, pl.ds(part, part)],
            send_sem=side_s.at[kind, stage, chunk],
            recv_sem=side_r.at[kind, stage, chunk],
            device_id=(target,),
            device_id_type=MESH,
        )

    barrier = pltpu.get_barrier_semaphore()
    for partner in (sibling, at(2), at(-2), far):
        pl.semaphore_signal(barrier, inc=1, device_id=(partner,), device_id_type=MESH)

    scale = s_ref[0]
    offset = b_ref[0]

    def normalise(kind, chunk):
        ref = (txt_ref, img_ref)[kind]
        for r in range(0, part, STRIP):
            full = ref[pl.ds(chunk * part + r, STRIP), :].astype(jnp.float32)
            length = jnp.sqrt(jnp.sum(full * full, axis=1, keepdims=True) + 1e-06)
            unit = (full * (1.0 / length)).astype(jnp.bfloat16)
            own[kind, pl.ds(chunk * part + r, STRIP), :] = unit
            buf[kind, 0, chunk, pl.ds(r, STRIP), :] = unit

    for chunk in range(CHUNKS):
        for kind in range(2):
            normalise(kind, chunk)
        if chunk == 0:
            pl.semaphore_wait(barrier, 4)
        for kind in range(2):
            chain(kind, 0, chunk).start()
            across(kind, 0, chunk, first_to[kind]).start()

    hat[...] = jnp.zeros_like(hat)
    losses[...] = jnp.zeros_like(losses)

    def unit_of(step):
        stage, chunk = step // CHUNKS, lax.rem(step, CHUNKS)
        row = lax.broadcasted_iota(jnp.int32, (rows, 2 * part), 0)
        col = lax.broadcasted_iota(jnp.int32, (rows, 2 * part), 1)
        shift = jnp.where(stage == 0, chunk * part, 2 * rows)
        same = (row == col + shift) & (col < part)
        for kind in range(2):
            across(kind, stage, chunk, sibling).wait_recv()
            scores = lax.dot_general(
                own[1 - kind], buf[kind, stage, chunk], (((1,), (1,)), ((), ())),
                preferred_element_type=jnp.float32,
            )
            logits = scale * scores + offset
            logits = jnp.where(same, -logits, logits)
            small = jnp.exp(-jnp.abs(logits))
            share = 1.0 / (1.0 + small)
            sig = jnp.where(logits >= 0, share, small * share)
            if kind == 0:
                losses[...] += jnp.maximum(logits, 0.0) + jnp.log1p(small)
            slope = jnp.where(same, -sig, sig).astype(jnp.bfloat16)
            for lane in range(0, depth, LANES):
                hat[1 - kind, :, pl.ds(lane, LANES)] += jnp.dot(
                    slope, buf[kind, stage, chunk, :, pl.ds(lane, LANES)],
                    preferred_element_type=jnp.float32,
                )

    def step_body(step, carry):
        stage, chunk = step // CHUNKS, lax.rem(step, CHUNKS)

        @pl.when(stage > 0)
        def _():
            for kind in range(2):
                chain(kind, stage - 1, chunk).wait_recv()

                @pl.when(stage < STAGES - 1)
                def _():
                    chain(kind, stage, chunk).start()

                across(kind, stage, chunk, sibling).start()

        @pl.when(step > 0)
        def _():
            unit_of(step - 1)

        return carry

    lax.fori_loop(0, STAGES * CHUNKS, step_body, 0)
    unit_of(jnp.int32(STAGES * CHUNKS - 1))

    loss_ref[...] = jnp.sum(losses[...].T, axis=0, keepdims=True) * (1.0 / (2 * STAGES * rows))
    for kind, ref, out in ((0, txt_ref, gt_ref), (1, img_ref, gi_ref)):
        def finish(i, carry, kind=kind, ref=ref, out=out):
            where = pl.ds(pl.multiple_of(i * STRIP, STRIP), STRIP)
            full = ref[where, :].astype(jnp.float32)
            length = jnp.sqrt(jnp.sum(full * full, axis=1, keepdims=True) + 1e-06)
            inverse = 1.0 / length
            unit = full * inverse
            total_hat = scale * hat[kind, where, :]
            along = jnp.sum(unit * total_hat, axis=1, keepdims=True)
            out[where, :] = (total_hat - unit * along) * inverse
            return carry

        lax.fori_loop(0, rows // STRIP, finish, 0)

    def drain(step, carry):
        stage, chunk = step // CHUNKS, lax.rem(step, CHUNKS)
        for kind in range(2):
            across(kind, stage, chunk, sibling).wait_send()

            @pl.when(stage < STAGES - 1)
            def _():
                chain(kind, stage, chunk).wait_send()

        return carry

    lax.fori_loop(0, STAGES * CHUNKS, drain, 0)


def on_device(picture_vectors, caption_vectors, sharpness_factor, affinity_offset):
    rows, depth = picture_vectors.shape
    part = rows // CHUNKS
    vmem = pl.BlockSpec(memory_space=pltpu.VMEM)
    smem = pl.BlockSpec(memory_space=pltpu.SMEM)
    loss, gi, gt = pl.pallas_call(
        kernel,
        name="window_loss",
        out_shape=(
            jax.ShapeDtypeStruct((1, rows), jnp.float32),
            jax.ShapeDtypeStruct((rows, depth), jnp.float32),
            jax.ShapeDtypeStruct((rows, depth), jnp.float32),
        ),
        in_specs=[smem, smem, vmem, vmem],
        out_specs=(vmem, vmem, vmem),
        scratch_shapes=[
            pltpu.VMEM((2, rows, depth), jnp.bfloat16),
            pltpu.VMEM((2, STAGES, CHUNKS, 2 * part, depth), jnp.bfloat16),
            pltpu.VMEM((2, rows, depth), jnp.float32),
            pltpu.VMEM((rows, 2 * part), jnp.float32),
            pltpu.SemaphoreType.DMA((2, STAGES, CHUNKS)),
            pltpu.SemaphoreType.DMA((2, STAGES, CHUNKS)),
            pltpu.SemaphoreType.DMA((2, STAGES, CHUNKS)),
            pltpu.SemaphoreType.DMA((2, STAGES, CHUNKS)),
        ],
        compiler_params=pltpu.CompilerParams(
            collective_id=0, has_side_effects=True, vmem_limit_bytes=48 * 2**20
        ),
        cost_estimate=pl.CostEstimate(
            flops=32 * 2 * rows * rows * depth, bytes_accessed=12 * rows * depth, transcendentals=32 * rows * rows
        ),
    )(sharpness_factor, affinity_offset, picture_vectors, caption_vectors)
    return loss.reshape(rows), gi, gt


def solution(mesh):
    placed = (P("dp", None), P("dp", None), P(), P())
    return jax.shard_map(
        on_device,
        mesh=mesh,
        in_specs=placed,
        out_specs=(P("dp"), P("dp", None), P("dp", None)),
        check_vma=False,
    )
```

time: 244 us -> 81.4 us (0.33)
  the two profiles are of different devices: /device:TPU:6 before, /device:TPU:342 now
where the time goes in v1:
time: 81.4 us; the launch traced here: 81.2 us
  Pallas kernels  74.5 us (92%)
  local copies, waits for them, and re-layouts  4.71 us (6%)
  between operations  1.94 us (2%)
    pallas_call x1, Pallas kernels, on_device(): pl.pallas_call(kernel, name='window_loss', out_shape=(jax.ShapeDtypeStruc...  74.5 us
    unnamed x7, local copies, waits for them, and re-layouts  4.71 us

profile of v1, /device:TPU:342, one launch (start us, length us, event | category | flops | bytes accessed | tf_op | source)
XLA Modules:
  0.0 81.2 jit_solution(17706330504113971645)
XLA Ops:
  1.9 0.0 copy-start
  1.9 1.1 %copy-done = bf16[256,1152]{1,0:T(8,128)(2,1)S(1)} copy-done((bf16[256,1152]{1,0:T(8,128)(2,1)S(1)}, bf16[256,1152]{1,0:T(8,128)(2,1)}, u32[]{:S(2)}) %copy-start) | copy-done | bytes 589848
  3.0 0.0 copy-start.1
  3.0 1.1 %copy-done.1 = bf16[256,1152]{1,0:T(8,128)(2,1)S(1)} copy-done((bf16[256,1152]{1,0:T(8,128)(2,1)S(1)}, bf16[256,1152]{1,0:T(8,128)(2,1)}, u32[]{:S(2)}) %copy-start.1) | copy-done | bytes 589848
  4.1 74.5 %window_loss.1 = (f32[1,256]{1,0:T(1,128)S(1)}, f32[256,1152]{1,0:T(8,128)S(1)}, f32[256,1152]{1,0:T(8,128)S(1)}) custom-call(f32[1]{0:T(128)S(6)} %copy.10.s_ref, f32[1]{0:T(128)S(6)} %copy.11.b_ref, bf16[256,1152]{1,0:T(8,128)(2,1)S(1)} %copy-done, bf16[256,1152]{1,0:T(8,128)(2,1)S(1)} %copy-done.1), custom_call_target="tpu_custom_call" | custom-call | flops 4831838208 | bytes 3538944 | tf_op jit(solution)/shard_map/window_loss/pallas_call | solution.py:165
  78.6 0.6 copy.12
  79.2 1.0 %copy.13 = f32[256,1152]{1,0:T(8,128)} copy(f32[256,1152]{1,0:T(8,128)S(1)} %get-tuple-element.13) | data formatting | bytes 2359296
  80.2 1.0 %copy.14 = f32[256,1152]{1,0:T(8,128)} copy(f32[256,1152]{1,0:T(8,128)S(1)} %get-tuple-element.14) | data formatting | bytes 2359296
Async XLA Ops:
  1.9 1.1 %copy-start = (bf16[256,1152]{1,0:T(8,128)(2,1)S(1)}, bf16[256,1152]{1,0:T(8,128)(2,1)}, u32[]{:S(2)}) copy-start(bf16[256,1152]{1,0:T(8,128)(2,1)} %img_ref.1) | copy-start | bytes 1769476
  3.0 1.1 %copy-start.1 = (bf16[256,1152]{1,0:T(8,128)(2,1)S(1)}, bf16[256,1152]{1,0:T(8,128)(2,1)}, u32[]{:S(2)}) copy-start(bf16[256,1152]{1,0:T(8,128)(2,1)} %txt_ref.1) | copy-start | bytes 1769476

commit v2 on v1

v2 whole, which is shorter than its diff:
```python
import jax
import jax.numpy as jnp
from jax import lax
from jax.experimental import pallas as pl
from jax.experimental.pallas import tpu as pltpu
from jax.sharding import PartitionSpec as P

WINDOW = 8
COLUMNS = 4
CHUNKS = 2
LANES = 384
STRIP = 32
TEXT, IMAGE = 0, 1
OWN, CROSS = 0, 1
RIGHT, LEFT = 0, 1
MESH = pl.DeviceIdType.MESH


def kernel(s_ref, b_ref, img_hbm, txt_hbm, loss_ref, gi_ref, gt_ref,
           raw, source, block, hat, losses, in_sem,
           row_s, row_r, hop_s, hop_r, relay_s, relay_r, pair_s, pair_r, row_ok, far_ok):
    rows, depth = raw.shape[1:]
    part = rows // CHUNKS
    n = lax.axis_index("dp")
    total = lax.axis_size("dp")
    core = lax.rem(n, 2)
    chip = n // 2
    column = lax.rem(chip, COLUMNS)
    row = chip // COLUMNS

    def at(offset):
        return lax.rem(n + offset + total, total)

    def in_row(offset):
        return (row * COLUMNS + lax.rem(column + offset + COLUMNS, COLUMNS)) * 2

    stride = 2 * COLUMNS
    sibling = n + 1 - 2 * core
    lead = n - core

    def lead_at(offset):
        return lax.rem(lead + offset + total, total)

    loads = [
        pltpu.make_async_copy(ref, raw.at[kind], in_sem.at[kind])
        for kind, ref in ((TEXT, txt_hbm), (IMAGE, img_hbm))
    ]
    for load in loads:
        load.start()

    barrier = pltpu.get_barrier_semaphore()

    def greet(device):
        pl.semaphore_signal(barrier, inc=1, device_id=(device,), device_id_type=MESH)

    greet(in_row(1))
    greet(in_row(-1))
    greet(lead_at(-stride))
    greet(lead_at(-2))
    greet(lead_at(stride) + 1)
    greet(lead_at(2) + 1)

    @pl.when(core == 1)
    def _():
        greet(sibling)

    def rows_of(chunk):
        return pl.ds(pl.multiple_of(chunk * part, part), part)

    mine = pl.ds(0, part)
    others = pl.ds(part, part)

    def copy(src, dst, send, recv, device):
        return pltpu.make_async_remote_copy(
            src_ref=src, dst_ref=dst, send_sem=send, recv_sem=recv, device_id=(device,), device_id_type=MESH
        )

    def to_row(kind, chunk):
        target = jnp.where(kind == TEXT, at(stride), at(-stride))
        return copy(source.at[kind, OWN, rows_of(chunk)], source.at[kind, CROSS, rows_of(chunk)],
                    row_s.at[kind, chunk], row_r.at[kind, chunk], target)

    def hop(kind, way, chunk, version):
        target = jnp.where(way == RIGHT, in_row(1), in_row(-1)) + core
        return copy(source.at[kind, version, rows_of(chunk)], block.at[1 + way, kind, chunk, mine],
                    hop_s.at[way, kind, chunk], hop_r.at[way, kind, chunk], target)

    def relay(kind, chunk):
        target = jnp.where(chunk == 1, at(2), at(-2))
        return copy(block.at[2 - chunk, kind, chunk, mine], block.at[3, kind, chunk, mine],
                    relay_s.at[kind, chunk], relay_r.at[kind, chunk], target)

    def across(group, kind, chunk, src):
        return copy(src, block.at[group, kind, chunk, others],
                    pair_s.at[group, kind, chunk], pair_r.at[group, kind, chunk], sibling)

    def sends_own(kind, way):
        first, last = column == 0, column == COLUMNS - 1
        return (
            (jnp.logical_not(last), first) if kind == TEXT else (last, jnp.logical_not(first))
        )[way]

    scale = s_ref[0]
    offset = b_ref[0]

    def normalise(kind, chunk):
        for r in range(0, part, STRIP):
            where = pl.ds(chunk * part + r, STRIP)
            full = raw[kind, where, :].astype(jnp.float32)
            length = jnp.sqrt(jnp.sum(full * full, axis=1, keepdims=True) + 1e-06)
            unit = (full * (1.0 / length)).astype(jnp.bfloat16)
            source[kind, OWN, where, :] = unit
            block[0, kind, chunk, pl.ds(r, STRIP), :] = unit

    for chunk in range(CHUNKS):
        for kind in (TEXT, IMAGE):
            if chunk == 0:
                loads[kind].wait()
            normalise(kind, chunk)
        if chunk == 0:
            @pl.when(core == 0)
            def _():
                pl.semaphore_wait(barrier, 9)
                pl.semaphore_signal(row_ok, inc=1, device_id=(sibling,), device_id_type=MESH)

            @pl.when(core == 1)
            def _():
                pl.semaphore_wait(row_ok, 1)

        for kind in (TEXT, IMAGE):
            for way in (RIGHT, LEFT):
                @pl.when(sends_own(kind, way))
                def _():
                    hop(kind, way, chunk, OWN).start()

        to_row(TEXT, chunk).start()

    hat[...] = jnp.zeros_like(hat)
    losses[...] = jnp.zeros_like(losses)

    @pl.when(core == 1)
    def _():
        pl.semaphore_wait(barrier, 4)
        pl.semaphore_signal(far_ok, inc=1, device_id=(sibling,), device_id_type=MESH)

    @pl.when(core == 0)
    def _():
        pl.semaphore_wait(far_ok, 1)

    for chunk in range(CHUNKS):
        to_row(IMAGE, chunk).start()

    early = (jnp.where(column == 0, IMAGE, TEXT), jnp.where(column == COLUMNS - 1, TEXT, IMAGE))
    relayed = (jnp.where(column == 1, IMAGE, TEXT), jnp.where(column == COLUMNS - 2, TEXT, IMAGE))

    def item(step):
        quarter, place = step // 4, lax.rem(step, 4)
        side, late = lax.rem(place, 2), place // 2
        group = jnp.where(quarter == 3, 3, jnp.where(quarter == 0, 0, 1 + side))
        first = jnp.where(side == 0, early[0], early[1])
        far = jnp.where(side == 0, relayed[0], relayed[1])
        kind = jnp.where(quarter == 0, 1 - side, jnp.where(quarter == 1, first, 1 - first))
        kind = jnp.where(quarter == 3, jnp.where(late == 0, far, 1 - far), kind)
        chunk = jnp.where(quarter == 3, 1 - side, late)
        return quarter, side, group, kind, chunk

    def arrival(step):
        quarter, side, group, kind, chunk = item(step)

        @pl.when(quarter == 0)
        def _():
            to_row(kind, chunk).wait_recv()
            for way in (RIGHT, LEFT):
                owned = jnp.where(kind == TEXT, sends_own(TEXT, way), sends_own(IMAGE, way))

                @pl.when(jnp.logical_not(owned))
                def _():
                    hop(kind, way, chunk, CROSS).start()

            version = jnp.where(kind == TEXT, core, 1 - core)
            across(0, kind, chunk, source.at[kind, version, rows_of(chunk)]).start()

        @pl.when(quarter > 0)
        def _():
            @pl.when(quarter < 3)
            def _():
                hop(kind, side, chunk, OWN).wait_recv()

                @pl.when(chunk == 1 - side)
                def _():
                    relay(kind, chunk).start()

            @pl.when(quarter == 3)
            def _():
                relay(kind, chunk).wait_recv()

            across(group, kind, chunk, block.at[group, kind, chunk, mine]).start()

    def work(step):
        _, _, group, kind, chunk = item(step)
        across(group, kind, chunk, block.at[group, kind, chunk, mine]).wait_recv()
        line = lax.broadcasted_iota(jnp.int32, (rows, 2 * part), 0)
        col = lax.broadcasted_iota(jnp.int32, (rows, 2 * part), 1)
        shift = jnp.where(group == 0, chunk * part, 2 * rows)
        same = (line == col + shift) & (col < part)
        scores = lax.dot_general(
            source[1 - kind, OWN], block[group, kind, chunk], (((1,), (1,)), ((), ())),
            preferred_element_type=jnp.float32,
        )
        logits = scale * scores + offset
        logits = jnp.where(same, -logits, logits)
        small = jnp.exp(-jnp.abs(logits))
        share = 1.0 / (1.0 + small)
        sig = jnp.where(logits >= 0, share, small * share)

        @pl.when(kind == TEXT)
        def _():
            losses[...] += jnp.maximum(logits, 0.0) + jnp.log1p(small)

        slope = jnp.where(same, -sig, sig).astype(jnp.bfloat16)
        for lane in range(0, depth, LANES):
            hat[1 - kind, :, pl.ds(lane, LANES)] += jnp.dot(
                slope, block[group, kind, chunk, :, pl.ds(lane, LANES)],
                preferred_element_type=jnp.float32,
            )

    def step_body(step, carry):
        @pl.when(step < 16)
        def _():
            arrival(step)

        @pl.when(step > 0)
        def _():
            work(step - 1)

        return carry

    lax.fori_loop(0, 17, step_body, 0)

    loss_ref[...] = jnp.sum(losses[...].T, axis=0, keepdims=True) * (1.0 / (WINDOW * rows))
    for kind, out in ((TEXT, gt_ref), (IMAGE, gi_ref)):
        def finish(i, carry, kind=kind, out=out):
            where = pl.ds(pl.multiple_of(i * STRIP, STRIP), STRIP)
            full = raw[kind, where, :].astype(jnp.float32)
            length = jnp.sqrt(jnp.sum(full * full, axis=1, keepdims=True) + 1e-06)
            inverse = 1.0 / length
            unit = full * inverse
            total_hat = scale * hat[kind, where, :]
            along = jnp.sum(unit * total_hat, axis=1, keepdims=True)
            out[where, :] = (total_hat - unit * along) * inverse
            return carry

        lax.fori_loop(0, rows // STRIP, finish, 0)

    def drain(step, carry):
        kind, chunk = step // CHUNKS, lax.rem(step, CHUNKS)
        to_row(kind, chunk).wait_send()
        for way in (RIGHT, LEFT):
            hop(kind, way, chunk, OWN).wait_send()
        relay(kind, chunk).wait_send()
        for group in range(4):
            across(group, kind, chunk, block.at[group, kind, chunk, mine]).wait_send()
        return carry

    lax.fori_loop(0, 2 * CHUNKS, drain, 0)


def on_device(picture_vectors, caption_vectors, sharpness_factor, affinity_offset):
    rows, depth = picture_vectors.shape
    part = rows // CHUNKS
    vmem = pl.BlockSpec(memory_space=pltpu.VMEM)
    smem = pl.BlockSpec(memory_space=pltpu.SMEM)
    anywhere = pl.BlockSpec(memory_space=pl.ANY)
    dma = pltpu.SemaphoreType.DMA
    loss, gi, gt = pl.pallas_call(
        kernel,
        name="window_loss",
        out_shape=(
            jax.ShapeDtypeStruct((1, rows), jnp.float32),
            jax.ShapeDtypeStruct((rows, depth), jnp.float32),
            jax.ShapeDtypeStruct((rows, depth), jnp.float32),
        ),
        in_specs=[smem, smem, anywhere, anywhere],
        out_specs=(vmem, vmem, vmem),
        scratch_shapes=[
            pltpu.VMEM((2, rows, depth), jnp.bfloat16),
            pltpu.VMEM((2, 2, rows, depth), jnp.bfloat16),
            pltpu.VMEM((4, 2, CHUNKS, 2 * part, depth), jnp.bfloat16),
            pltpu.VMEM((2, rows, depth), jnp.float32),
            pltpu.VMEM((rows, 2 * part), jnp.float32),
            dma((2,)),
            dma((2, CHUNKS)), dma((2, CHUNKS)),
            dma((2, 2, CHUNKS)), dma((2, 2, CHUNKS)),
            dma((2, CHUNKS)), dma((2, CHUNKS)),
            dma((4, 2, CHUNKS)), dma((4, 2, CHUNKS)),
            pltpu.SemaphoreType.REGULAR, pltpu.SemaphoreType.REGULAR,
        ],
        compiler_params=pltpu.CompilerParams(
            collective_id=0, has_side_effects=True, vmem_limit_bytes=48 * 2**20
        ),
        cost_estimate=pl.CostEstimate(
            flops=32 * 2 * rows * rows * depth, bytes_accessed=12 * rows * depth, transcendentals=32 * rows * rows
        ),
    )(sharpness_factor, affinity_offset, picture_vectors, caption_vectors)
    return loss.reshape(rows), gi, gt


def solution(mesh):
    placed = (P("dp", None), P("dp", None), P(), P())
    return jax.shard_map(
        on_device,
        mesh=mesh,
        in_specs=placed,
        out_specs=(P("dp"), P("dp", None), P("dp", None)),
        check_vma=False,
    )
```

time: 81.4 us -> 69 us (0.85)
  the two profiles are of different devices: /device:TPU:342 before, /device:TPU:1 now
where the time goes in v2:
time: 69 us; the launch traced here: 68.8 us
  Pallas kernels  62.2 us (90%)
  local copies, waits for them, and re-layouts  4.71 us (7%)
  between operations  1.94 us (3%)
    pallas_call x1, Pallas kernels, on_device(): pl.pallas_call(kernel, name='window_loss', out_shape=(jax.ShapeDtypeStruc...  62.2 us
    unnamed x7, local copies, waits for them, and re-layouts  4.71 us

profile of v2, /device:TPU:1, one launch (start us, length us, event | category | flops | bytes accessed | tf_op | source)
XLA Modules:
  0.0 68.8 jit_solution(17816961338311829786)
XLA Ops:
  1.9 0.0 copy-start
  1.9 1.1 %copy-done = bf16[256,1152]{1,0:T(8,128)(2,1)S(1)} copy-done((bf16[256,1152]{1,0:T(8,128)(2,1)S(1)}, bf16[256,1152]{1,0:T(8,128)(2,1)}, u32[]{:S(2)}) %copy-start) | copy-done | bytes 589848
  3.0 0.0 copy-start.1
  3.0 1.1 %copy-done.1 = bf16[256,1152]{1,0:T(8,128)(2,1)S(1)} copy-done((bf16[256,1152]{1,0:T(8,128)(2,1)S(1)}, bf16[256,1152]{1,0:T(8,128)(2,1)}, u32[]{:S(2)}) %copy-start.1) | copy-done | bytes 589848
  4.1 62.2 %window_loss.1 = (f32[1,256]{1,0:T(1,128)S(1)}, f32[256,1152]{1,0:T(8,128)S(1)}, f32[256,1152]{1,0:T(8,128)S(1)}) custom-call(f32[1]{0:T(128)S(6)} %copy.10.s_ref, f32[1]{0:T(128)S(6)} %copy.11.b_ref, bf16[256,1152]{1,0:T(8,128)(2,1)S(1)} %copy-done, bf16[256,1152]{1,0:T(8,128)(2,1)S(1)} %copy-done.1), custom_call_target="tpu_custom_call" | custom-call | flops 4831838208 | bytes 3538944 | tf_op jit(solution)/shard_map/window_loss/pallas_call | solution.py:275
  66.2 0.6 copy.12
  66.8 1.0 %copy.13 = f32[256,1152]{1,0:T(8,128)} copy(f32[256,1152]{1,0:T(8,128)S(1)} %get-tuple-element.13) | data formatting | bytes 2359296
  67.8 1.0 %copy.14 = f32[256,1152]{1,0:T(8,128)} copy(f32[256,1152]{1,0:T(8,128)S(1)} %get-tuple-element.14) | data formatting | bytes 2359296
Async XLA Ops:
  1.9 1.1 %copy-start = (bf16[256,1152]{1,0:T(8,128)(2,1)S(1)}, bf16[256,1152]{1,0:T(8,128)(2,1)}, u32[]{:S(2)}) copy-start(bf16[256,1152]{1,0:T(8,128)(2,1)} %img_hbm.1) | copy-start | bytes 1769476
  3.0 1.1 %copy-start.1 = (bf16[256,1152]{1,0:T(8,128)(2,1)S(1)}, bf16[256,1152]{1,0:T(8,128)(2,1)}, u32[]{:S(2)}) copy-start(bf16[256,1152]{1,0:T(8,128)(2,1)} %txt_hbm.1) | copy-start | bytes 1769476

commit v3 on v2

--- a/solution.py
+++ b/solution.py
@@ -10,15 +10,21 @@
 CHUNKS = 2
 LANES = 384
 STRIP = 32
+PIECES = 4
+NARROW = 16
+ORDER = (
+    (0, 1, 1), (1, 0, 1), (1, 1, 0), (0, 0, 0), (0, 1, 0), (0, 0, 1), (1, 0, 0), (1, 1, 1),
+    (2, 0, 1), (2, 1, 0), (2, 0, 0), (2, 1, 1), (3, 0, 1), (3, 1, 0), (3, 0, 1), (3, 1, 0),
+)
 TEXT, IMAGE = 0, 1
 OWN, CROSS = 0, 1
 RIGHT, LEFT = 0, 1
 MESH = pl.DeviceIdType.MESH
 
 
-def kernel(s_ref, b_ref, img_hbm, txt_hbm, loss_ref, gi_ref, gt_ref,
-           raw, source, block, hat, losses, in_sem,
-           row_s, row_r, hop_s, hop_r, relay_s, relay_r, pair_s, pair_r, row_ok, far_ok):
+def window_kernel(s_ref, b_ref, img_hbm, txt_hbm, raw, hat, losses, inverses,
+                  source, block, turned, in_sem, row_s, row_r, hop_s, hop_r, relay_s, relay_r, turn_s, turn_r,
+                  pair_s, pair_r, row_ok, far_ok):
     rows, depth = raw.shape[1:]
     part = rows // CHUNKS
     n = lax.axis_index("dp")
@@ -56,9 +62,7 @@
     greet(in_row(1))
     greet(in_row(-1))
     greet(lead_at(-stride))
-    greet(lead_at(-2))
     greet(lead_at(stride) + 1)
-    greet(lead_at(2) + 1)
 
     @pl.when(core == 1)
     def _():
@@ -85,10 +89,26 @@
         return copy(source.at[kind, version, rows_of(chunk)], block.at[1 + way, kind, chunk, mine],
                     hop_s.at[way, kind, chunk], hop_r.at[way, kind, chunk], target)
 
-    def relay(kind, chunk):
-        target = jnp.where(chunk == 1, at(2), at(-2))
-        return copy(block.at[2 - chunk, kind, chunk, mine], block.at[3, kind, chunk, mine],
-                    relay_s.at[kind, chunk], relay_r.at[kind, chunk], target)
+    def relay(way, kind, chunk):
+        return copy(block.at[1 + way, kind, chunk, mine], block.at[3, kind, chunk, mine],
+                    relay_s.at[way, kind, chunk], relay_r.at[kind, chunk], beside(way))
+
+    def beside(way):
+        return jnp.where(way == RIGHT, in_row(1), in_row(-1)) + core
+
+    ends = (column == COLUMNS - 1) | (column == 0)
+    end_way = jnp.where(column == COLUMNS - 1, RIGHT, LEFT)
+    end_kind = jnp.where(column == COLUMNS - 1, TEXT, IMAGE)
+    upper = column >= COLUMNS // 2
+
+    def turn(chunk):
+        target = jnp.where(column == COLUMNS - 1, at(stride), at(-stride))
+        return copy(block.at[1 + end_way, end_kind, chunk, mine], turned.at[chunk],
+                    turn_s.at[chunk], turn_r.at[chunk], target)
+
+    def relay_turned(chunk):
+        return copy(turned.at[chunk], block.at[3, end_kind, chunk, mine],
+                    relay_s.at[end_way, end_kind, chunk], relay_r.at[end_kind, chunk], beside(end_way))
 
     def across(group, kind, chunk, src):
         return copy(src, block.at[group, kind, chunk, others],
@@ -107,10 +127,17 @@
         for r in range(0, part, STRIP):
             where = pl.ds(chunk * part + r, STRIP)
             full = raw[kind, where, :].astype(jnp.float32)
-            length = jnp.sqrt(jnp.sum(full * full, axis=1, keepdims=True) + 1e-06)
-            unit = (full * (1.0 / length)).astype(jnp.bfloat16)
+            inverse = 1.0 / jnp.sqrt(jnp.sum(full * full, axis=1, keepdims=True) + 1e-06)
+            inverses[kind, where, :] = jnp.broadcast_to(inverse, (STRIP, 128))
+            unit = (full * inverse).astype(jnp.bfloat16)
             source[kind, OWN, where, :] = unit
             block[0, kind, chunk, pl.ds(r, STRIP), :] = unit
+
+    def own_hops(way, chunk):
+        for kind in (TEXT, IMAGE):
+            @pl.when(sends_own(kind, way))
+            def _():
+                hop(kind, way, chunk, OWN).start()
 
     for chunk in range(CHUNKS):
         for kind in (TEXT, IMAGE):
@@ -120,19 +147,17 @@
         if chunk == 0:
             @pl.when(core == 0)
             def _():
-                pl.semaphore_wait(barrier, 9)
+                pl.semaphore_wait(barrier, 7)
                 pl.semaphore_signal(row_ok, inc=1, device_id=(sibling,), device_id_type=MESH)
 
             @pl.when(core == 1)
             def _():
                 pl.semaphore_wait(row_ok, 1)
 
-        for kind in (TEXT, IMAGE):
-            for way in (RIGHT, LEFT):
-                @pl.when(sends_own(kind, way))
-                def _():
-                    hop(kind, way, chunk, OWN).start()
-
+        if chunk == 0:
+            own_hops(LEFT, 0)
+        else:
+            own_hops(RIGHT, 1)
         to_row(TEXT, chunk).start()
 
     hat[...] = jnp.zeros_like(hat)
@@ -140,34 +165,47 @@
 
     @pl.when(core == 1)
     def _():
-        pl.semaphore_wait(barrier, 4)
+        pl.semaphore_wait(barrier, 2)
         pl.semaphore_signal(far_ok, inc=1, device_id=(sibling,), device_id_type=MESH)
 
     @pl.when(core == 0)
     def _():
         pl.semaphore_wait(far_ok, 1)
 
-    for chunk in range(CHUNKS):
+    for chunk in (1, 0):
         to_row(IMAGE, chunk).start()
+    own_hops(RIGHT, 0)
+    own_hops(LEFT, 1)
 
     early = (jnp.where(column == 0, IMAGE, TEXT), jnp.where(column == COLUMNS - 1, TEXT, IMAGE))
-    relayed = (jnp.where(column == 1, IMAGE, TEXT), jnp.where(column == COLUMNS - 2, TEXT, IMAGE))
+    nearer = jnp.where(upper, TEXT, IMAGE)
+
+    def pick(step, values):
+        code = 0
+        for i, value in enumerate(values):
+            code = code + value * (step == i).astype(jnp.int32)
+        return code
 
     def item(step):
-        quarter, place = step // 4, lax.rem(step, 4)
-        side, late = lax.rem(place, 2), place // 2
-        group = jnp.where(quarter == 3, 3, jnp.where(quarter == 0, 0, 1 + side))
+        stage = pick(step, [s for s, _, _ in ORDER])
+        side = pick(step, [s for _, s, _ in ORDER])
+        chunk = pick(step, [s for _, _, s in ORDER])
+        group = jnp.where(stage == 3, 3, jnp.where(stage == 0, 0, 1 + side))
         first = jnp.where(side == 0, early[0], early[1])
-        far = jnp.where(side == 0, relayed[0], relayed[1])
-        kind = jnp.where(quarter == 0, 1 - side, jnp.where(quarter == 1, first, 1 - first))
-        kind = jnp.where(quarter == 3, jnp.where(late == 0, far, 1 - far), kind)
-        chunk = jnp.where(quarter == 3, 1 - side, late)
-        return quarter, side, group, kind, chunk
+        kind = jnp.where(stage == 0, side, jnp.where(stage == 1, first, 1 - first))
+        kind = jnp.where(stage == 3, jnp.where(step < 14, nearer, 1 - nearer), kind)
+        return stage, side, group, kind, chunk
 
     def arrival(step):
-        quarter, side, group, kind, chunk = item(step)
-
-        @pl.when(quarter == 0)
+        stage, side, group, kind, chunk = item(step)
+
+        for when, half in ((8, 1 - end_way), (10, end_way)):
+            @pl.when(ends & (step == when))
+            def _():
+                turn(half).wait_recv()
+                relay_turned(half).start()
+
+        @pl.when(stage == 0)
         def _():
             to_row(kind, chunk).wait_recv()
             for way in (RIGHT, LEFT):
@@ -180,19 +218,27 @@
             version = jnp.where(kind == TEXT, core, 1 - core)
             across(0, kind, chunk, source.at[kind, version, rows_of(chunk)]).start()
 
-        @pl.when(quarter > 0)
-        def _():
-            @pl.when(quarter < 3)
+        @pl.when(stage > 0)
+        def _():
+            @pl.when(stage < 3)
             def _():
                 hop(kind, side, chunk, OWN).wait_recv()
 
-                @pl.when(chunk == 1 - side)
+                whole = (side == RIGHT) == upper
+                passes = jnp.where(whole, (kind == side).astype(jnp.int32), (chunk == 1 - side).astype(jnp.int32)) == 1
+                turns = ends & (side == end_way)
+
+                @pl.when(passes & jnp.logical_not(turns))
                 def _():
-                    relay(kind, chunk).start()
-
-            @pl.when(quarter == 3)
-            def _():
-                relay(kind, chunk).wait_recv()
+                    relay(side, kind, chunk).start()
+
+                @pl.when(passes & turns)
+                def _():
+                    turn(chunk).start()
+
+            @pl.when(stage == 3)
+            def _():
+                relay(RIGHT, kind, chunk).wait_recv()
 
             across(group, kind, chunk, block.at[group, kind, chunk, mine]).start()
 
@@ -237,32 +283,53 @@
 
     lax.fori_loop(0, 17, step_body, 0)
 
-    loss_ref[...] = jnp.sum(losses[...].T, axis=0, keepdims=True) * (1.0 / (WINDOW * rows))
-    for kind, out in ((TEXT, gt_ref), (IMAGE, gi_ref)):
-        def finish(i, carry, kind=kind, out=out):
-            where = pl.ds(pl.multiple_of(i * STRIP, STRIP), STRIP)
-            full = raw[kind, where, :].astype(jnp.float32)
-            length = jnp.sqrt(jnp.sum(full * full, axis=1, keepdims=True) + 1e-06)
-            inverse = 1.0 / length
-            unit = full * inverse
-            total_hat = scale * hat[kind, where, :]
-            along = jnp.sum(unit * total_hat, axis=1, keepdims=True)
-            out[where, :] = (total_hat - unit * along) * inverse
-            return carry
-
-        lax.fori_loop(0, rows // STRIP, finish, 0)
-
     def drain(step, carry):
         kind, chunk = step // CHUNKS, lax.rem(step, CHUNKS)
         to_row(kind, chunk).wait_send()
         for way in (RIGHT, LEFT):
             hop(kind, way, chunk, OWN).wait_send()
-        relay(kind, chunk).wait_send()
         for group in range(4):
             across(group, kind, chunk, block.at[group, kind, chunk, mine]).wait_send()
+
         return carry
 
     lax.fori_loop(0, 2 * CHUNKS, drain, 0)
+    relay(RIGHT, TEXT, 1).wait_send()
+    relay(LEFT, IMAGE, 0).wait_send()
+    lower = 1 - upper.astype(jnp.int32)
+    relay(RIGHT, lower, lower).wait_send()
+    relay(LEFT, lower, lower).wait_send()
+
+    @pl.when(ends)
+    def _():
+        for chunk in range(CHUNKS):
+            turn(chunk).wait_send()
+
+
+def project_kernel(s_ref, raw, hat, losses, inverses, loss_ref, gi_hbm, gt_hbm, result, sem):
+    rows, depth = raw.shape[1:]
+    size = rows // PIECES
+    scale = s_ref[0]
+    copies = []
+    for kind, out in ((TEXT, gt_hbm), (IMAGE, gi_hbm)):
+        for piece in range(PIECES):
+            for r in range(0, size, NARROW):
+                where = pl.ds(piece * size + r, NARROW)
+                along = jnp.sum(raw[kind, where, :].astype(jnp.float32) * hat[kind, where, :], axis=1, keepdims=True)
+                inverse = inverses[kind, where, :]
+                outer = scale * inverse
+                inner = outer * inverse * inverse * along
+                for lane in range(0, depth, 128):
+                    lanes = pl.ds(lane, 128)
+                    result[kind, where, lanes] = (
+                        outer * hat[kind, where, lanes] - inner * raw[kind, where, lanes].astype(jnp.float32)
+                    )
+            span = pl.ds(piece * size, size)
+            copies.append(pltpu.make_async_copy(result.at[kind, span], out.at[span], sem.at[kind, piece]))
+            copies[-1].start()
+    loss_ref[...] = jnp.sum(losses[...].T, axis=0, keepdims=True) * (1.0 / (WINDOW * rows))
+    for one in copies:
+        one.wait()
 
 
 def on_device(picture_vectors, caption_vectors, sharpness_factor, affinity_offset):
@@ -270,28 +337,28 @@
     part = rows // CHUNKS
     vmem = pl.BlockSpec(memory_space=pltpu.VMEM)
     smem = pl.BlockSpec(memory_space=pltpu.SMEM)
-    anywhere = pl.BlockSpec(memory_space=pl.ANY)
+    anywhere = pl.BlockSpec(memory_space=pltpu.HBM)
     dma = pltpu.SemaphoreType.DMA
-    loss, gi, gt = pl.pallas_call(
-        kernel,
+    raw, hat, losses, inverses = pl.pallas_call(
+        window_kernel,
         name="window_loss",
         out_shape=(
-            jax.ShapeDtypeStruct((1, rows), jnp.float32),
-            jax.ShapeDtypeStruct((rows, depth), jnp.float32),
-            jax.ShapeDtypeStruct((rows, depth), jnp.float32),
+            jax.ShapeDtypeStruct((2, rows, depth), jnp.bfloat16),
+            jax.ShapeDtypeStruct((2, rows, depth), jnp.float32),
+            jax.ShapeDtypeStruct((rows, 2 * part), jnp.float32),
+            jax.ShapeDtypeStruct((2, rows, 128), jnp.float32),
         ),
         in_specs=[smem, smem, anywhere, anywhere],
-        out_specs=(vmem, vmem, vmem),
+        out_specs=(vmem, vmem, vmem, vmem),
         scratch_shapes=[
-            pltpu.VMEM((2, rows, depth), jnp.bfloat16),
             pltpu.VMEM((2, 2, rows, depth), jnp.bfloat16),
             pltpu.VMEM((4, 2, CHUNKS, 2 * part, depth), jnp.bfloat16),
-            pltpu.VMEM((2, rows, depth), jnp.float32),
-            pltpu.VMEM((rows, 2 * part), jnp.float32),
+            pltpu.VMEM((CHUNKS, part, depth), jnp.bfloat16),
             dma((2,)),
             dma((2, CHUNKS)), dma((2, CHUNKS)),
             dma((2, 2, CHUNKS)), dma((2, 2, CHUNKS)),
-            dma((2, CHUNKS)), dma((2, CHUNKS)),
+            dma((2, 2, CHUNKS)), dma((2, CHUNKS)),
+            dma((CHUNKS,)), dma((CHUNKS,)),
             dma((4, 2, CHUNKS)), dma((4, 2, CHUNKS)),
             pltpu.SemaphoreType.REGULAR, pltpu.SemaphoreType.REGULAR,
         ],
@@ -302,6 +369,19 @@
             flops=32 * 2 * rows * rows * depth, bytes_accessed=12 * rows * depth, transcendentals=32 * rows * rows
         ),
     )(sharpness_factor, affinity_offset, picture_vectors, caption_vectors)
+    loss, gi, gt = pl.pallas_call(
+        project_kernel,
+        name="projection",
+        out_shape=(
+            jax.ShapeDtypeStruct((1, rows), jnp.float32),
+            jax.ShapeDtypeStruct((rows, depth), jnp.float32),
+            jax.ShapeDtypeStruct((rows, depth), jnp.float32),
+        ),
+        in_specs=[smem, vmem, vmem, vmem, vmem],
+        out_specs=(vmem, anywhere, anywhere),
+        scratch_shapes=[pltpu.VMEM((2, rows, depth), jnp.float32), dma((2, PIECES))],
+        compiler_params=pltpu.CompilerParams(vmem_limit_bytes=16 * 2**20),
+    )(sharpness_factor, raw, hat, losses, inverses)
     return loss.reshape(rows), gi, gt
 
 

time: 69 us -> 62.7 us (0.909)
  Pallas kernels: 62.2 us -> 58.4 us
  local copies, waits for them, and re-layouts: 4.71 us -> 2.12 us
    pallas_call x1 -> x2, Pallas kernels: 62.2 us -> 58.4 us  [the longest x1 56.1 us: on_device(): pl.pallas_call(window_kernel, name='window_loss', out_shape=(jax.ShapeDty...]
    unnamed x7 -> x4, local copies, waits for them, and re-layouts: 4.71 us -> 2.12 us
where the time goes in v3:
time: 62.7 us; the launch traced here: 62.5 us
  Pallas kernels  58.4 us (93%)
  local copies, waits for them, and re-layouts  2.12 us (3%)
  between operations  1.94 us (3%)
    pallas_call x1, Pallas kernels, on_device(): pl.pallas_call(window_kernel, name='window_loss', out_shape=(jax.ShapeDty...  56.1 us
    pallas_call x1, Pallas kernels, on_device(): pl.pallas_call(project_kernel, name='projection', out_shape=(jax.ShapeDty...  2.29 us
    unnamed x4, local copies, waits for them, and re-layouts  2.12 us

profile of v3, /device:TPU:1, one launch (start us, length us, event | category | flops | bytes accessed | tf_op | source)
XLA Modules:
  0.0 62.5 jit_solution(17545462991938922087)
XLA Ops:
  1.9 0.0 copy-start
  1.9 1.1 %copy-done = bf16[256,1152]{1,0:T(8,128)(2,1)S(1)} copy-done((bf16[256,1152]{1,0:T(8,128)(2,1)S(1)}, bf16[256,1152]{1,0:T(8,128)(2,1)}, u32[]{:S(2)}) %copy-start) | copy-done | bytes 589848
  3.0 0.0 copy-start.1
  3.0 1.1 %copy-done.1 = bf16[256,1152]{1,0:T(8,128)(2,1)S(1)} copy-done((bf16[256,1152]{1,0:T(8,128)(2,1)S(1)}, bf16[256,1152]{1,0:T(8,128)(2,1)}, u32[]{:S(2)}) %copy-start.1) | copy-done | bytes 589848
  4.1 56.1 %window_loss.1 = (bf16[2,256,1152]{2,1,0:T(8,128)(2,1)S(1)}, f32[2,256,1152]{2,1,0:T(8,128)S(1)}, f32[256,256]{1,0:T(8,128)S(1)}, f32[2,256,128]{2,1,0:T(8,128)S(1)}) custom-call(f32[1]{0:T(128)S(6)} %copy.7.s_ref, f32[1]{0:T(128)S(6)} %copy.8.b_ref, bf16[256,1152]{1,0:T(8,128)(2,1)S(1)} %copy-done, bf16[256,1152]{1,0:T(8,128)(2,1)S(1)} %copy-done.1), custom_call_target="tpu_custom_call" | custom-call | flops 4831838208 | bytes 3538944 | tf_op jit(solution)/shard_map/window_loss/pallas_call | solution.py:342
  60.2 2.3 %projection.1 = (f32[1,256]{1,0:T(1,128)}, f32[256,1152]{1,0:T(8,128)}, f32[256,1152]{1,0:T(8,128)}) custom-call(f32[1]{0:T(128)S(6)} %copy.7.s_ref, bf16[2,256,1152]{2,1,0:T(8,128)(2,1)S(1)} %get-tuple-element.10.raw, f32[2,256,1152]{2,1,0:T(8,128)S(1)} %get-tuple-element.11.hat, f32[256,256]{1,0:T(8,128)S(1)} %get-tuple-element.12.losses, ...), custom_call_target="tpu_custom_call" | custom-call | tf_op jit(solution)/shard_map/projection/pallas_call | solution.py:372
Async XLA Ops:
  1.9 1.1 %copy-start = (bf16[256,1152]{1,0:T(8,128)(2,1)S(1)}, bf16[256,1152]{1,0:T(8,128)(2,1)}, u32[]{:S(2)}) copy-start(bf16[256,1152]{1,0:T(8,128)(2,1)} %img_hbm.1) | copy-start | bytes 1769476
  3.0 1.1 %copy-start.1 = (bf16[256,1152]{1,0:T(8,128)(2,1)S(1)}, bf16[256,1152]{1,0:T(8,128)(2,1)}, u32[]{:S(2)}) copy-start(bf16[256,1152]{1,0:T(8,128)(2,1)} %txt_hbm.1) | copy-start | bytes 1769476

commit v4 on v3

--- a/solution.py
+++ b/solution.py
@@ -12,6 +12,7 @@
 STRIP = 32
 PIECES = 4
 NARROW = 16
+LAG = 3
 ORDER = (
     (0, 1, 1), (1, 0, 1), (1, 1, 0), (0, 0, 0), (0, 1, 0), (0, 0, 1), (1, 0, 0), (1, 1, 1),
     (2, 0, 1), (2, 1, 0), (2, 0, 0), (2, 1, 1), (3, 0, 1), (3, 1, 0), (3, 0, 1), (3, 1, 0),
@@ -22,10 +23,10 @@
 MESH = pl.DeviceIdType.MESH
 
 
-def window_kernel(s_ref, b_ref, img_hbm, txt_hbm, raw, hat, losses, inverses,
-                  source, block, turned, in_sem, row_s, row_r, hop_s, hop_r, relay_s, relay_r, turn_s, turn_r,
-                  pair_s, pair_r, row_ok, far_ok):
-    rows, depth = raw.shape[1:]
+def window_kernel(s_ref, b_ref, img_ref, txt_ref, hat, losses, inverses,
+                  source, block, turned, row_s, row_r, hop_s, hop_r, relay_s, relay_r, turn_s, turn_r,
+                  pair_s, pair_r, pair_ok, far_ok):
+    rows, depth = img_ref.shape
     part = rows // CHUNKS
     n = lax.axis_index("dp")
     total = lax.axis_size("dp")
@@ -42,27 +43,15 @@
 
     stride = 2 * COLUMNS
     sibling = n + 1 - 2 * core
-    lead = n - core
-
-    def lead_at(offset):
-        return lax.rem(lead + offset + total, total)
-
-    loads = [
-        pltpu.make_async_copy(ref, raw.at[kind], in_sem.at[kind])
-        for kind, ref in ((TEXT, txt_hbm), (IMAGE, img_hbm))
-    ]
-    for load in loads:
-        load.start()
 
     barrier = pltpu.get_barrier_semaphore()
 
     def greet(device):
         pl.semaphore_signal(barrier, inc=1, device_id=(device,), device_id_type=MESH)
 
-    greet(in_row(1))
-    greet(in_row(-1))
-    greet(lead_at(-stride))
-    greet(lead_at(stride) + 1)
+    greet(in_row(1) + core)
+    greet(in_row(-1) + core)
+    greet(at(-stride))
 
     @pl.when(core == 1)
     def _():
@@ -126,7 +115,7 @@
     def normalise(kind, chunk):
         for r in range(0, part, STRIP):
             where = pl.ds(chunk * part + r, STRIP)
-            full = raw[kind, where, :].astype(jnp.float32)
+            full = (txt_ref, img_ref)[kind][where, :].astype(jnp.float32)
             inverse = 1.0 / jnp.sqrt(jnp.sum(full * full, axis=1, keepdims=True) + 1e-06)
             inverses[kind, where, :] = jnp.broadcast_to(inverse, (STRIP, 128))
             unit = (full * inverse).astype(jnp.bfloat16)
@@ -141,18 +130,18 @@
 
     for chunk in range(CHUNKS):
         for kind in (TEXT, IMAGE):
-            if chunk == 0:
-                loads[kind].wait()
             normalise(kind, chunk)
         if chunk == 0:
             @pl.when(core == 0)
             def _():
-                pl.semaphore_wait(barrier, 7)
-                pl.semaphore_signal(row_ok, inc=1, device_id=(sibling,), device_id_type=MESH)
+                pl.semaphore_wait(barrier, 4)
+                pl.semaphore_signal(pair_ok, inc=1, device_id=(sibling,), device_id_type=MESH)
 
             @pl.when(core == 1)
             def _():
-                pl.semaphore_wait(row_ok, 1)
+                pl.semaphore_wait(barrier, 3)
+
+            pl.semaphore_signal(far_ok, inc=1, device_id=(at(stride),), device_id_type=MESH)
 
         if chunk == 0:
             own_hops(LEFT, 0)
@@ -160,22 +149,18 @@
             own_hops(RIGHT, 1)
         to_row(TEXT, chunk).start()
 
+    own_hops(RIGHT, 0)
+    own_hops(LEFT, 1)
     hat[...] = jnp.zeros_like(hat)
     losses[...] = jnp.zeros_like(losses)
 
+    pl.semaphore_wait(far_ok, 1)
+    for chunk in (1, 0):
+        to_row(IMAGE, chunk).start()
+
     @pl.when(core == 1)
     def _():
-        pl.semaphore_wait(barrier, 2)
-        pl.semaphore_signal(far_ok, inc=1, device_id=(sibling,), device_id_type=MESH)
-
-    @pl.when(core == 0)
-    def _():
-        pl.semaphore_wait(far_ok, 1)
-
-    for chunk in (1, 0):
-        to_row(IMAGE, chunk).start()
-    own_hops(RIGHT, 0)
-    own_hops(LEFT, 1)
+        pl.semaphore_wait(pair_ok, 1)
 
     early = (jnp.where(column == 0, IMAGE, TEXT), jnp.where(column == COLUMNS - 1, TEXT, IMAGE))
     nearer = jnp.where(upper, TEXT, IMAGE)
@@ -255,13 +240,12 @@
         )
         logits = scale * scores + offset
         logits = jnp.where(same, -logits, logits)
-        small = jnp.exp(-jnp.abs(logits))
-        share = 1.0 / (1.0 + small)
-        sig = jnp.where(logits >= 0, share, small * share)
+        power = jnp.exp(logits)
+        sig = power / (1.0 + power)
 
         @pl.when(kind == TEXT)
         def _():
-            losses[...] += jnp.maximum(logits, 0.0) + jnp.log1p(small)
+            losses[...] += jnp.log1p(power)
 
         slope = jnp.where(same, -sig, sig).astype(jnp.bfloat16)
         for lane in range(0, depth, LANES):
@@ -270,15 +254,15 @@
                 preferred_element_type=jnp.float32,
             )
 
+    def done(step):
+        return jnp.where(step < 12, jnp.maximum(step - LAG + 1, 0), jnp.minimum(13 - LAG + 2 * (step - 12), step))
+
     def step_body(step, carry):
         @pl.when(step < 16)
         def _():
             arrival(step)
 
-        @pl.when(step > 0)
-        def _():
-            work(step - 1)
-
+        lax.fori_loop(done(step - 1), done(step), lambda i, c: (work(i), c)[1], 0)
         return carry
 
     lax.fori_loop(0, 17, step_body, 0)
@@ -306,23 +290,23 @@
             turn(chunk).wait_send()
 
 
-def project_kernel(s_ref, raw, hat, losses, inverses, loss_ref, gi_hbm, gt_hbm, result, sem):
-    rows, depth = raw.shape[1:]
+def project_kernel(s_ref, img_ref, txt_ref, hat, losses, inverses, loss_ref, gi_hbm, gt_hbm, result, sem):
+    rows, depth = img_ref.shape
     size = rows // PIECES
     scale = s_ref[0]
     copies = []
-    for kind, out in ((TEXT, gt_hbm), (IMAGE, gi_hbm)):
+    for kind, raw, out in ((TEXT, txt_ref, gt_hbm), (IMAGE, img_ref, gi_hbm)):
         for piece in range(PIECES):
             for r in range(0, size, NARROW):
                 where = pl.ds(piece * size + r, NARROW)
-                along = jnp.sum(raw[kind, where, :].astype(jnp.float32) * hat[kind, where, :], axis=1, keepdims=True)
+                along = jnp.sum(raw[where, :].astype(jnp.float32) * hat[kind, where, :], axis=1, keepdims=True)
                 inverse = inverses[kind, where, :]
                 outer = scale * inverse
                 inner = outer * inverse * inverse * along
                 for lane in range(0, depth, 128):
                     lanes = pl.ds(lane, 128)
                     result[kind, where, lanes] = (
-                        outer * hat[kind, where, lanes] - inner * raw[kind, where, lanes].astype(jnp.float32)
+                        outer * hat[kind, where, lanes] - inner * raw[where, lanes].astype(jnp.float32)
                     )
             span = pl.ds(piece * size, size)
             copies.append(pltpu.make_async_copy(result.at[kind, span], out.at[span], sem.at[kind, piece]))
@@ -339,22 +323,20 @@
     smem = pl.BlockSpec(memory_space=pltpu.SMEM)
     anywhere = pl.BlockSpec(memory_space=pltpu.HBM)
     dma = pltpu.SemaphoreType.DMA
-    raw, hat, losses, inverses = pl.pallas_call(
+    hat, losses, inverses = pl.pallas_call(
         window_kernel,
         name="window_loss",
         out_shape=(
-            jax.ShapeDtypeStruct((2, rows, depth), jnp.bfloat16),
             jax.ShapeDtypeStruct((2, rows, depth), jnp.float32),
             jax.ShapeDtypeStruct((rows, 2 * part), jnp.float32),
             jax.ShapeDtypeStruct((2, rows, 128), jnp.float32),
         ),
-        in_specs=[smem, smem, anywhere, anywhere],
-        out_specs=(vmem, vmem, vmem, vmem),
+        in_specs=[smem, smem, vmem, vmem],
+        out_specs=(vmem, vmem, vmem),
         scratch_shapes=[
             pltpu.VMEM((2, 2, rows, depth), jnp.bfloat16),
             pltpu.VMEM((4, 2, CHUNKS, 2 * part, depth), jnp.bfloat16),
             pltpu.VMEM((CHUNKS, part, depth), jnp.bfloat16),
-            dma((2,)),
             dma((2, CHUNKS)), dma((2, CHUNKS)),
             dma((2, 2, CHUNKS)), dma((2, 2, CHUNKS)),
             dma((2, 2, CHUNKS)), dma((2, CHUNKS)),
@@ -377,11 +359,11 @@
             jax.ShapeDtypeStruct((rows, depth), jnp.float32),
             jax.ShapeDtypeStruct((rows, depth), jnp.float32),
         ),
-        in_specs=[smem, vmem, vmem, vmem, vmem],
+        in_specs=[smem, vmem, vmem, vmem, vmem, vmem],
         out_specs=(vmem, anywhere, anywhere),
         scratch_shapes=[pltpu.VMEM((2, rows, depth), jnp.float32), dma((2, PIECES))],
         compiler_params=pltpu.CompilerParams(vmem_limit_bytes=16 * 2**20),
-    )(sharpness_factor, raw, hat, losses, inverses)
+    )(sharpness_factor, picture_vectors, caption_vectors, hat, losses, inverses)
     return loss.reshape(rows), gi, gt
 
 

time: 62.7 us -> 59.8 us (0.954)
  Pallas kernels: 58.4 us -> 55.1 us
    pallas_call x1, Pallas kernels: 56.1 us -> 52.8 us  [on_device(): pl.pallas_call(window_kernel, name='window_loss', out_shape=(jax.ShapeDty...]
where the time goes in v4:
time: 59.8 us; the launch traced here: 59.2 us
  Pallas kernels  55.1 us (92%)
  local copies, waits for them, and re-layouts  2.12 us (4%)
  between operations  1.94 us (3%)
    pallas_call x1, Pallas kernels, on_device(): pl.pallas_call(window_kernel, name='window_loss', out_shape=(jax.ShapeDty...  52.8 us
    pallas_call x1, Pallas kernels, on_device(): pl.pallas_call(project_kernel, name='projection', out_shape=(jax.ShapeDty...  2.29 us
    unnamed x4, local copies, waits for them, and re-layouts  2.12 us

profile of v4, /device:TPU:1, one launch (start us, length us, event | category | flops | bytes accessed | tf_op | source)
XLA Modules:
  0.0 59.2 jit_solution(869318024051434016)
XLA Ops:
  1.9 0.0 copy-start
  1.9 1.1 %copy-done = bf16[256,1152]{1,0:T(8,128)(2,1)S(1)} copy-done((bf16[256,1152]{1,0:T(8,128)(2,1)S(1)}, bf16[256,1152]{1,0:T(8,128)(2,1)}, u32[]{:S(2)}) %copy-start) | copy-done | bytes 589848
  3.0 0.0 copy-start.1
  3.0 1.1 %copy-done.1 = bf16[256,1152]{1,0:T(8,128)(2,1)S(1)} copy-done((bf16[256,1152]{1,0:T(8,128)(2,1)S(1)}, bf16[256,1152]{1,0:T(8,128)(2,1)}, u32[]{:S(2)}) %copy-start.1) | copy-done | bytes 589848
  4.1 52.8 %window_loss.1 = (f32[2,256,1152]{2,1,0:T(8,128)S(1)}, f32[256,256]{1,0:T(8,128)S(1)}, f32[2,256,128]{2,1,0:T(8,128)S(1)}) custom-call(f32[1]{0:T(128)S(6)} %copy.7.s_ref, f32[1]{0:T(128)S(6)} %copy.8.b_ref, bf16[256,1152]{1,0:T(8,128)(2,1)S(1)} %copy-done, bf16[256,1152]{1,0:T(8,128)(2,1)S(1)} %copy-done.1), custom_call_target="tpu_custom_call" | custom-call | flops 4831838208 | bytes 3538944 | tf_op jit(solution)/shard_map/window_loss/pallas_call | solution.py:326
  56.9 2.3 %projection.1 = (f32[1,256]{1,0:T(1,128)}, f32[256,1152]{1,0:T(8,128)}, f32[256,1152]{1,0:T(8,128)}) custom-call(f32[1]{0:T(128)S(6)} %copy.7.s_ref, bf16[256,1152]{1,0:T(8,128)(2,1)S(1)} %copy-done, bf16[256,1152]{1,0:T(8,128)(2,1)S(1)} %copy-done.1, f32[2,256,1152]{2,1,0:T(8,128)S(1)} %get-tuple-element.9.hat, f32[256,256]{1,0:T(8,128)S(1)} %get-tuple-element.10.losses, ...), custom_call_target="tpu_custom_call" | custom-call | tf_op jit(solution)/shard_map/projection/pallas_call | solution.py:354
Async XLA Ops:
  1.9 1.1 %copy-start = (bf16[256,1152]{1,0:T(8,128)(2,1)S(1)}, bf16[256,1152]{1,0:T(8,128)(2,1)}, u32[]{:S(2)}) copy-start(bf16[256,1152]{1,0:T(8,128)(2,1)} %img_ref.3) | copy-start | bytes 1769476
  3.0 1.1 %copy-start.1 = (bf16[256,1152]{1,0:T(8,128)(2,1)S(1)}, bf16[256,1152]{1,0:T(8,128)(2,1)}, u32[]{:S(2)}) copy-start(bf16[256,1152]{1,0:T(8,128)(2,1)} %txt_ref.3) | copy-start | bytes 1769476

commit v5 on v4

--- a/solution.py
+++ b/solution.py
@@ -8,11 +8,11 @@
 WINDOW = 8
 COLUMNS = 4
 CHUNKS = 2
-LANES = 384
+LANES = 1152
 STRIP = 32
 PIECES = 4
 NARROW = 16
-LAG = 3
+DONE = (0, 0, 0, 1, 2, 3, 4, 5, 6, 8, 9, 11, 12, 13, 14, 15, 16)
 ORDER = (
     (0, 1, 1), (1, 0, 1), (1, 1, 0), (0, 0, 0), (0, 1, 0), (0, 0, 1), (1, 0, 0), (1, 1, 1),
     (2, 0, 1), (2, 1, 0), (2, 0, 0), (2, 1, 1), (3, 0, 1), (3, 1, 0), (3, 0, 1), (3, 1, 0),
@@ -255,7 +255,7 @@
             )
 
     def done(step):
-        return jnp.where(step < 12, jnp.maximum(step - LAG + 1, 0), jnp.minimum(13 - LAG + 2 * (step - 12), step))
+        return pick(step, DONE)
 
     def step_body(step, carry):
         @pl.when(step < 16)

time: 59.8 us -> 59.1 us (0.988)
  no operation moved by 1% of the time
where the time goes in v5:
time: 59.1 us; the launch traced here: 58.9 us
  Pallas kernels  54.8 us (93%)
  local copies, waits for them, and re-layouts  2.12 us (4%)
  between operations  1.94 us (3%)
    pallas_call x1, Pallas kernels, on_device(): pl.pallas_call(window_kernel, name='window_loss', out_shape=(jax.ShapeDty...  52.5 us
    pallas_call x1, Pallas kernels, on_device(): pl.pallas_call(project_kernel, name='projection', out_shape=(jax.ShapeDty...  2.29 us
    unnamed x4, local copies, waits for them, and re-layouts  2.12 us

profile of v5, /device:TPU:1, one launch (start us, length us, event | category | flops | bytes accessed | tf_op | source)
XLA Modules:
  0.0 58.9 jit_solution(3706803096975683173)
XLA Ops:
  1.9 0.0 copy-start
  1.9 1.1 %copy-done = bf16[256,1152]{1,0:T(8,128)(2,1)S(1)} copy-done((bf16[256,1152]{1,0:T(8,128)(2,1)S(1)}, bf16[256,1152]{1,0:T(8,128)(2,1)}, u32[]{:S(2)}) %copy-start) | copy-done | bytes 589848
  3.0 0.0 copy-start.1
  3.0 1.1 %copy-done.1 = bf16[256,1152]{1,0:T(8,128)(2,1)S(1)} copy-done((bf16[256,1152]{1,0:T(8,128)(2,1)S(1)}, bf16[256,1152]{1,0:T(8,128)(2,1)}, u32[]{:S(2)}) %copy-start.1) | copy-done | bytes 589848
  4.1 52.5 %window_loss.1 = (f32[2,256,1152]{2,1,0:T(8,128)S(1)}, f32[256,256]{1,0:T(8,128)S(1)}, f32[2,256,128]{2,1,0:T(8,128)S(1)}) custom-call(f32[1]{0:T(128)S(6)} %copy.7.s_ref, f32[1]{0:T(128)S(6)} %copy.8.b_ref, bf16[256,1152]{1,0:T(8,128)(2,1)S(1)} %copy-done, bf16[256,1152]{1,0:T(8,128)(2,1)S(1)} %copy-done.1), custom_call_target="tpu_custom_call" | custom-call | flops 4831838208 | bytes 3538944 | tf_op jit(solution)/shard_map/window_loss/pallas_call | solution.py:326
  56.6 2.3 %projection.1 = (f32[1,256]{1,0:T(1,128)}, f32[256,1152]{1,0:T(8,128)}, f32[256,1152]{1,0:T(8,128)}) custom-call(f32[1]{0:T(128)S(6)} %copy.7.s_ref, bf16[256,1152]{1,0:T(8,128)(2,1)S(1)} %copy-done, bf16[256,1152]{1,0:T(8,128)(2,1)S(1)} %copy-done.1, f32[2,256,1152]{2,1,0:T(8,128)S(1)} %get-tuple-element.9.hat, f32[256,256]{1,0:T(8,128)S(1)} %get-tuple-element.10.losses, ...), custom_call_target="tpu_custom_call" | custom-call | tf_op jit(solution)/shard_map/projection/pallas_call | solution.py:354
Async XLA Ops:
  1.9 1.1 %copy-start = (bf16[256,1152]{1,0:T(8,128)(2,1)S(1)}, bf16[256,1152]{1,0:T(8,128)(2,1)}, u32[]{:S(2)}) copy-start(bf16[256,1152]{1,0:T(8,128)(2,1)} %img_ref.3) | copy-start | bytes 1769476
  3.0 1.1 %copy-start.1 = (bf16[256,1152]{1,0:T(8,128)(2,1)S(1)}, bf16[256,1152]{1,0:T(8,128)(2,1)}, u32[]{:S(2)}) copy-start(bf16[256,1152]{1,0:T(8,128)(2,1)} %txt_ref.3) | copy-start | bytes 1769476

commit v6 on v5

--- a/solution.py
+++ b/solution.py
@@ -12,7 +12,7 @@
 STRIP = 32
 PIECES = 4
 NARROW = 16
-DONE = (0, 0, 0, 1, 2, 3, 4, 5, 6, 8, 9, 11, 12, 13, 14, 15, 16)
+DONE = (0, 0, 0, 1, 2, 3, 4, 5, 7, 9, 10, 11, 12, 13, 14, 15, 16)
 ORDER = (
     (0, 1, 1), (1, 0, 1), (1, 1, 0), (0, 0, 0), (0, 1, 0), (0, 0, 1), (1, 0, 0), (1, 1, 1),
     (2, 0, 1), (2, 1, 0), (2, 0, 0), (2, 1, 1), (3, 0, 1), (3, 1, 0), (3, 0, 1), (3, 1, 0),
@@ -151,8 +151,6 @@
 
     own_hops(RIGHT, 0)
     own_hops(LEFT, 1)
-    hat[...] = jnp.zeros_like(hat)
-    losses[...] = jnp.zeros_like(losses)
 
     pl.semaphore_wait(far_ok, 1)
     for chunk in (1, 0):
@@ -161,6 +159,9 @@
     @pl.when(core == 1)
     def _():
         pl.semaphore_wait(pair_ok, 1)
+
+    hat[...] = jnp.zeros_like(hat)
+    losses[...] = jnp.zeros_like(losses)
 
     early = (jnp.where(column == 0, IMAGE, TEXT), jnp.where(column == COLUMNS - 1, TEXT, IMAGE))
     nearer = jnp.where(upper, TEXT, IMAGE)

time: 59.1 us -> 59.1 us (level)
  no operation moved by 1% of the time
where the time goes in v6:
time: 59.1 us; the launch traced here: 58.9 us
  Pallas kernels  54.8 us (93%)
  local copies, waits for them, and re-layouts  2.12 us (4%)
  between operations  1.94 us (3%)
    pallas_call x1, Pallas kernels, on_device(): pl.pallas_call(window_kernel, name='window_loss', out_shape=(jax.ShapeDty...  52.5 us
    pallas_call x1, Pallas kernels, on_device(): pl.pallas_call(project_kernel, name='projection', out_shape=(jax.ShapeDty...  2.29 us
    unnamed x4, local copies, waits for them, and re-layouts  2.12 us

profile of v6, /device:TPU:1, one launch (start us, length us, event | category | flops | bytes accessed | tf_op | source)
XLA Modules:
  0.0 58.9 jit_solution(8059755814665608437)
XLA Ops:
  1.9 0.0 copy-start
  1.9 1.1 %copy-done = bf16[256,1152]{1,0:T(8,128)(2,1)S(1)} copy-done((bf16[256,1152]{1,0:T(8,128)(2,1)S(1)}, bf16[256,1152]{1,0:T(8,128)(2,1)}, u32[]{:S(2)}) %copy-start) | copy-done | bytes 589848
  3.0 0.0 copy-start.1
  3.0 1.1 %copy-done.1 = bf16[256,1152]{1,0:T(8,128)(2,1)S(1)} copy-done((bf16[256,1152]{1,0:T(8,128)(2,1)S(1)}, bf16[256,1152]{1,0:T(8,128)(2,1)}, u32[]{:S(2)}) %copy-start.1) | copy-done | bytes 589848
  4.1 52.5 %window_loss.1 = (f32[2,256,1152]{2,1,0:T(8,128)S(1)}, f32[256,256]{1,0:T(8,128)S(1)}, f32[2,256,128]{2,1,0:T(8,128)S(1)}) custom-call(f32[1]{0:T(128)S(6)} %copy.7.s_ref, f32[1]{0:T(128)S(6)} %copy.8.b_ref, bf16[256,1152]{1,0:T(8,128)(2,1)S(1)} %copy-done, bf16[256,1152]{1,0:T(8,128)(2,1)S(1)} %copy-done.1), custom_call_target="tpu_custom_call" | custom-call | flops 4831838208 | bytes 3538944 | tf_op jit(solution)/shard_map/window_loss/pallas_call | solution.py:327
  56.6 2.3 %projection.1 = (f32[1,256]{1,0:T(1,128)}, f32[256,1152]{1,0:T(8,128)}, f32[256,1152]{1,0:T(8,128)}) custom-call(f32[1]{0:T(128)S(6)} %copy.7.s_ref, bf16[256,1152]{1,0:T(8,128)(2,1)S(1)} %copy-done, bf16[256,1152]{1,0:T(8,128)(2,1)S(1)} %copy-done.1, f32[2,256,1152]{2,1,0:T(8,128)S(1)} %get-tuple-element.9.hat, f32[256,256]{1,0:T(8,128)S(1)} %get-tuple-element.10.losses, ...), custom_call_target="tpu_custom_call" | custom-call | tf_op jit(solution)/shard_map/projection/pallas_call | solution.py:355
Async XLA Ops:
  1.9 1.1 %copy-start = (bf16[256,1152]{1,0:T(8,128)(2,1)S(1)}, bf16[256,1152]{1,0:T(8,128)(2,1)}, u32[]{:S(2)}) copy-start(bf16[256,1152]{1,0:T(8,128)(2,1)} %img_ref.3) | copy-start | bytes 1769476
  3.0 1.1 %copy-start.1 = (bf16[256,1152]{1,0:T(8,128)(2,1)S(1)}, bf16[256,1152]{1,0:T(8,128)(2,1)}, u32[]{:S(2)}) copy-start(bf16[256,1152]{1,0:T(8,128)(2,1)} %txt_ref.3) | copy-start | bytes 1769476
